TPU v7x, 256 devices: a whole 4x4x8 slice. The times are simulated.
256 devices in a mesh: tiles: 64 (over x, z, core), comp: 4 (over y).
Axes of the slice: x: 4, y: 4, z: 8, core: 2. Of those that a mesh axis runs over, the one named last changes fastest.
Arguments:
- action: float32 [768, 32768], P('comp', 'tiles'), may hold values from 0 to 4
- speed_courant: float32 [32], replicated, may hold values from 0.15 to 0.6
- turning: float32 [32768], P('tiles'), may hold values from -0.45 to 0.45
- freq_shift: float32 [32768], P('tiles'), may hold values from -0.45 to 0.45
- wind_speed: float32 [32768], P('tiles'), may hold values from 0.1 to 1.2
- wind_dir: float32 [32768], P('tiles'), may hold values from -3.140625 to 3.140625
- sea_mask: int32 [32768], P('tiles'), may hold values 0 or 1
- neighbours: int32 [4, 32768], P(None, 'tiles'), may hold values from 0 to 768
- halo_rows: int32 [16384], P('tiles'), may hold values from 0 to 511
Outputs:
- updated: float32 [768, 32768], P('comp', 'tiles')
All inputs are finite; a program needn't handle non-finite values. No bound on the sum of `sea_mask` on one device may be relied on, other than what follows from the above.
Results may differ from a plain program's by a relative error of at most 0.0003.
Values sent between devices are 32-bit elements; how exact they have to be, the bound alone decides.
A program may use at most 64 MiB of HBM per device.

v0:
```python
import math

import jax
import jax.numpy as jnp
from jax import lax
from jax.sharding import PartitionSpec as P

NSUB = 4


def extended_2(x, sides, width):
    for axis, dim in sides:
        size, length = (lax.axis_size(axis), x.shape[dim])
        up = [(i, (i + 1) % size) for i in range(size - 1)]
        down = [(j, i) for i, j in up]
        last = lax.slice_in_dim(x, length - width, length, axis=dim)
        first = lax.slice_in_dim(x, 0, width, axis=dim)
        before = lax.ppermute(last, axis, up)
        after = lax.ppermute(first, axis, down)
        x = jnp.concatenate([before, x, after], axis=dim)
    return x


def sigma_table(freqs):
    offsets = (jnp.arange(freqs) - freqs // 2).astype(jnp.float32)
    return jnp.exp(offsets * jnp.float32(math.log(1.1)))


def advect_rows(spectrum, left_rim, right_rim, neighbours, wet_column, speed_x, speed_y):
    used = left_rim.shape[0] + spectrum.shape[0] + right_rim.shape[0]
    filler = used + 1 + -(used + 1) % 8 - used
    empty_rows = jnp.zeros((filler, spectrum.shape[1]), jnp.float32)
    extended = jnp.concatenate([left_rim, spectrum, right_rim, empty_rows], axis=0)
    from_west = jnp.take(extended, neighbours[0], axis=0)
    from_east = jnp.take(extended, neighbours[1], axis=0)
    from_south = jnp.take(extended, neighbours[2], axis=0)
    from_north = jnp.take(extended, neighbours[3], axis=0)
    upwind_x = jnp.where(speed_x > 0, from_west, from_east)
    upwind_y = jnp.where(speed_y > 0, from_south, from_north)
    return wet_column * (
        spectrum
        - jnp.abs(speed_x) * (spectrum - upwind_x)
        - jnp.abs(speed_y) * (spectrum - upwind_y)
    )


def refract(spectrum, before, beyond, turning):
    rate = turning[None, None, :]
    return spectrum - jnp.abs(rate) * (spectrum - jnp.where(rate > 0, before, beyond))


def shift_freq(spectrum, shifting):
    empty_row = jnp.zeros_like(spectrum[:, :1])
    lower_freq = jnp.concatenate([empty_row, spectrum[:, :-1]], axis=1)
    upper_freq = jnp.concatenate([spectrum[:, 1:], empty_row], axis=1)
    rate = shifting[None, None, :]
    return spectrum - jnp.abs(rate) * (spectrum - jnp.where(rate > 0, lower_freq, upper_freq))


def apply_sources(shifted, energy, moment, angles, sigmas, speed, direction, wet_points):
    mean_freq = moment / jnp.maximum(energy, 0.05)
    sigcol = sigmas[None, :, None]
    damping = (
        0.005
        * (sigcol * sigcol)
        * (mean_freq * mean_freq * mean_freq * energy * energy)[None, None, :]
    )
    aligned = jnp.cos(angles[:, None, None] - direction[None, None, :])
    growth = 0.4 * jnp.maximum(speed[None, None, :] * sigcol * aligned - 0.3, 0.0)
    return wet_points * shifted * (1.0 + growth) / (1.0 + damping)


def sources(spectrum, turning, shifting, speed, direction, wet_points, angles, sigmas, comps):
    before = jnp.roll(spectrum, 1, axis=0)
    beyond = jnp.roll(spectrum, -1, axis=0)
    refracted = refract(spectrum, before, beyond, turning)
    shifted = shift_freq(refracted, shifting)
    energy = jnp.sum(shifted * sigmas[None, :, None], axis=(0, 1)) / comps
    moment = jnp.sum(shifted * (sigmas * sigmas)[None, :, None], axis=(0, 1)) / comps
    return apply_sources(shifted, energy, moment, angles, sigmas, speed, direction, wet_points)


def shards(
    action,
    speed_courant,
    turning,
    freq_shift,
    wind_speed,
    wind_dir,
    sea_mask,
    neighbours,
    halo_rows,
):
    comp_count = lax.axis_size("comp")
    comp_index = lax.axis_index("comp")
    comp_rows, points = action.shape
    freqs = speed_courant.shape[0]
    directions = comp_rows // freqs
    total_dirs = directions * comp_count
    comps = comp_rows * comp_count
    rim_width = halo_rows.shape[0] // 2
    wet_points = sea_mask.astype(jnp.float32)
    step_angle = jnp.float32(2.0 * math.pi / total_dirs)
    local_angles = (comp_index * directions + jnp.arange(directions)).astype(
        jnp.float32
    ) * step_angle
    speed_x = (speed_courant[None, :] * jnp.cos(local_angles)[:, None]).reshape(1, comp_rows)
    speed_y = (speed_courant[None, :] * jnp.sin(local_angles)[:, None]).reshape(1, comp_rows)
    wet_column = wet_points[:, None]
    by_point = jnp.transpose(action) * wet_column
    for substep in range(NSUB):
        outgoing = jnp.take(by_point, halo_rows, axis=0)
        received = extended_2(outgoing, (("tiles", 0),), rim_width)
        left_rim = received[:rim_width]
        right_rim = received[3 * rim_width :]
        by_point = advect_rows(
            by_point, left_rim, right_rim, neighbours, wet_column, speed_x, speed_y
        )
    spectrum = jnp.transpose(by_point).reshape(directions, freqs, points)
    sigmas = sigma_table(freqs)
    quarter = points // comp_count
    by_owner = spectrum.reshape(comp_rows, comp_count, quarter)
    at_points = lax.all_to_all(by_owner, "comp", split_axis=1, concat_axis=0, tiled=True).reshape(
        total_dirs, freqs, quarter
    )
    offset = comp_index * quarter
    all_angles = jnp.arange(total_dirs).astype(jnp.float32) * step_angle
    result = sources(
        at_points,
        lax.dynamic_slice_in_dim(turning, offset, quarter),
        lax.dynamic_slice_in_dim(freq_shift, offset, quarter),
        lax.dynamic_slice_in_dim(wind_speed, offset, quarter),
        lax.dynamic_slice_in_dim(wind_dir, offset, quarter),
        lax.dynamic_slice_in_dim(wet_points, offset, quarter),
        all_angles,
        sigmas,
        comps,
    )
    returned = lax.all_to_all(
        result.reshape(comps, 1, quarter), "comp", split_axis=0, concat_axis=1, tiled=True
    )
    return returned.reshape(comp_rows, points)


def solution(mesh):
    placed = (
        P("comp", "tiles"),
        P(),
        P("tiles"),
        P("tiles"),
        P("tiles"),
        P("tiles"),
        P("tiles"),
        P(None, "tiles"),
        P("tiles"),
    )
    return jax.shard_map(
        shards, mesh=mesh, in_specs=placed, out_specs=P("comp", "tiles"), check_vma=False
    )
```

profile of v0, /device:TPU:6, one launch (start us, length us, event | category | flops | bytes accessed | tf_op | source)
XLA Modules:
  0.0 107.7 jit_solution(16124453834426232015)
XLA Ops:
  3.2 1.9 %collective-permute-start = (f32[128,192]{0,1:T(8,128)S(1)}, f32[128,192]{0,1:T(8,128)S(1)}, u32[]{:S(2)}, u32[]{:S(2)}) collective-permute-start(f32[128,192]{0,1:T(8,128)S(1)} %get-tuple-element.22), channel_id=1, source_target_pairs={{0,4},{4,8},{8,12},{12,16},{16,20},{20,24},{24,28},{28,32},{32,36}... | collective-permute-start | bytes 294920 | tf_op jit(solution)/shard_map/ppermute | solution.py:18
  5.1 7.5 %collective-permute-start.1 = (f32[128,192]{0,1:T(8,128)S(1)}, f32[128,192]{0,1:T(8,128)S(1)}, u32[]{:S(2)}, u32[]{:S(2)}) collective-permute-start(f32[128,192]{0,1:T(8,128)S(1)} %get-tuple-element.23), channel_id=1, source_target_pairs={{4,0},{8,4},{12,8},{16,12},{20,16},{24,20},{28,24},{32,28},{36,32}... | collective-permute-start | bytes 294920 | tf_op jit(solution)/shard_map/ppermute | solution.py:19
  16.7 1.6 %gather_fusion.1 = f32[512,192]{1,0:T(8,128)S(1)} fusion(f32[776,192]{1,0:T(8,128)S(1)} %copy.22, s32[1024]{0:T(1024)S(1)} %pad_clamp_fusion.3), kind=kCustom, calls=%fused_computation.1.clone | custom fusion | bytes 788480 | tf_op jit(solution)/shard_map/jit(_take)/gather | solution.py:34
  18.4 1.6 %gather_fusion.2 = f32[512,192]{1,0:T(8,128)S(1)} fusion(f32[776,192]{1,0:T(8,128)S(1)} %copy.22, s32[1024]{0:T(1024)S(1)} %pad_clamp_fusion.2), kind=kCustom, calls=%fused_computation.5.clone | custom fusion | bytes 788480 | tf_op jit(solution)/shard_map/jit(_take)/gather | solution.py:35
  20.2 1.6 %gather_fusion.3 = f32[512,192]{1,0:T(8,128)S(1)} fusion(f32[776,192]{1,0:T(8,128)S(1)} %copy.22, s32[1024]{0:T(1024)S(1)} %pad_clamp_fusion.1), kind=kCustom, calls=%fused_computation.6.clone | custom fusion | bytes 788480 | tf_op jit(solution)/shard_map/jit(_take)/gather | solution.py:36
  22.0 1.6 %gather_fusion.4 = f32[512,192]{1,0:T(8,128)S(1)} fusion(f32[776,192]{1,0:T(8,128)S(1)} %copy.22, s32[1024]{0:T(1024)S(1)} %pad_clamp_fusion), kind=kCustom, calls=%fused_computation.7.clone | custom fusion | bytes 788480 | tf_op jit(solution)/shard_map/jit(_take)/gather | solution.py:37
  26.2 1.9 %collective-permute-start.2 = (f32[128,192]{0,1:T(8,128)S(1)}, f32[128,192]{0,1:T(8,128)S(1)}, u32[]{:S(2)}, u32[]{:S(2)}) collective-permute-start(f32[128,192]{0,1:T(8,128)S(1)} %get-tuple-element.20), channel_id=1, source_target_pairs={{0,4},{4,8},{8,12},{12,16},{16,20},{20,24},{24,28},{28,32},{32,36}... | collective-permute-start | bytes 294920 | tf_op jit(solution)/shard_map/ppermute | solution.py:18
  28.1 5.8 %collective-permute-start.3 = (f32[128,192]{0,1:T(8,128)S(1)}, f32[128,192]{0,1:T(8,128)S(1)}, u32[]{:S(2)}, u32[]{:S(2)}) collective-permute-start(f32[128,192]{0,1:T(8,128)S(1)} %get-tuple-element.21), channel_id=1, source_target_pairs={{4,0},{8,4},{12,8},{16,12},{20,16},{24,20},{28,24},{32,28},{36,32}... | collective-permute-start | bytes 294920 | tf_op jit(solution)/shard_map/ppermute | solution.py:19
  34.3 1.8 %collective-permute-done.3 = f32[128,192]{0,1:T(8,128)S(1)} collective-permute-done((f32[128,192]{0,1:T(8,128)S(1)}, f32[128,192]{0,1:T(8,128)S(1)}, u32[]{:S(2)}, u32[]{:S(2)}) %collective-permute-start.3) | collective-permute-done | bytes 98336 | tf_op jit(solution)/shard_map/ppermute | solution.py:19
  36.4 1.6 %gather_fusion.6 = f32[512,192]{1,0:T(8,128)S(1)} fusion(f32[776,192]{1,0:T(8,128)S(1)} %copy.32, s32[1024]{0:T(1024)S(1)} %pad_clamp_fusion.3), kind=kCustom, calls=%fused_computation.8.clone | custom fusion | bytes 788480 | tf_op jit(solution)/shard_map/jit(_take)/gather | solution.py:34
  38.0 1.6 %gather_fusion.7 = f32[512,192]{1,0:T(8,128)S(1)} fusion(f32[776,192]{1,0:T(8,128)S(1)} %copy.32, s32[1024]{0:T(1024)S(1)} %pad_clamp_fusion.2), kind=kCustom, calls=%fused_computation.9.clone | custom fusion | bytes 788480 | tf_op jit(solution)/shard_map/jit(_take)/gather | solution.py:35
  39.6 1.6 %gather_fusion.8 = f32[512,192]{1,0:T(8,128)S(1)} fusion(f32[776,192]{1,0:T(8,128)S(1)} %copy.32, s32[1024]{0:T(1024)S(1)} %pad_clamp_fusion.1), kind=kCustom, calls=%fused_computation.10.clone | custom fusion | bytes 788480 | tf_op jit(solution)/shard_map/jit(_take)/gather | solution.py:36
  41.2 1.6 %gather_fusion.9 = f32[512,192]{1,0:T(8,128)S(1)} fusion(f32[776,192]{1,0:T(8,128)S(1)} %copy.32, s32[1024]{0:T(1024)S(1)} %pad_clamp_fusion), kind=kCustom, calls=%fused_computation.11.clone | custom fusion | bytes 788480 | tf_op jit(solution)/shard_map/jit(_take)/gather | solution.py:37
  45.2 1.9 %collective-permute-start.4 = (f32[128,192]{0,1:T(8,128)S(1)}, f32[128,192]{0,1:T(8,128)S(1)}, u32[]{:S(2)}, u32[]{:S(2)}) collective-permute-start(f32[128,192]{0,1:T(8,128)S(1)} %get-tuple-element.18), channel_id=1, source_target_pairs={{0,4},{4,8},{8,12},{12,16},{16,20},{20,24},{24,28},{28,32},{32,36}... | collective-permute-start | bytes 294920 | tf_op jit(solution)/shard_map/ppermute | solution.py:18
  47.1 6.0 %collective-permute-start.5 = (f32[128,192]{0,1:T(8,128)S(1)}, f32[128,192]{0,1:T(8,128)S(1)}, u32[]{:S(2)}, u32[]{:S(2)}) collective-permute-start(f32[128,192]{0,1:T(8,128)S(1)} %get-tuple-element.19), channel_id=1, source_target_pairs={{4,0},{8,4},{12,8},{16,12},{20,16},{24,20},{28,24},{32,28},{36,32}... | collective-permute-start | bytes 294920 | tf_op jit(solution)/shard_map/ppermute | solution.py:19
  53.3 1.8 %collective-permute-done.5 = f32[128,192]{0,1:T(8,128)S(1)} collective-permute-done((f32[128,192]{0,1:T(8,128)S(1)}, f32[128,192]{0,1:T(8,128)S(1)}, u32[]{:S(2)}, u32[]{:S(2)}) %collective-permute-start.5) | collective-permute-done | bytes 98336 | tf_op jit(solution)/shard_map/ppermute | solution.py:19
  55.5 2.2 %gather_fusion.11 = f32[512,192]{1,0:T(8,128)} fusion(f32[776,192]{1,0:T(8,128)S(1)} %copy.42, s32[1024]{0:T(1024)S(1)} %pad_clamp_fusion.3), kind=kCustom, calls=%fused_computation.12.clone | custom fusion | bytes 788480 | tf_op jit(solution)/shard_map/jit(_take)/gather | solution.py:34
  57.7 1.6 %gather_fusion.12 = f32[512,192]{1,0:T(8,128)S(1)} fusion(f32[776,192]{1,0:T(8,128)S(1)} %copy.42, s32[1024]{0:T(1024)S(1)} %pad_clamp_fusion.2), kind=kCustom, calls=%fused_computation.13.clone | custom fusion | bytes 788480 | tf_op jit(solution)/shard_map/jit(_take)/gather | solution.py:35
  59.3 1.6 %gather_fusion.13 = f32[512,192]{1,0:T(8,128)S(1)} fusion(f32[776,192]{1,0:T(8,128)S(1)} %copy.42, s32[1024]{0:T(1024)S(1)} %pad_clamp_fusion.1), kind=kCustom, calls=%fused_computation.14.clone | custom fusion | bytes 788480 | tf_op jit(solution)/shard_map/jit(_take)/gather | solution.py:36
  60.9 1.6 %gather_fusion.14 = f32[512,192]{1,0:T(8,128)S(1)} fusion(f32[776,192]{1,0:T(8,128)S(1)} %copy.42, s32[1024]{0:T(1024)S(1)} %pad_clamp_fusion), kind=kCustom, calls=%fused_computation.15.clone | custom fusion | bytes 788480 | tf_op jit(solution)/shard_map/jit(_take)/gather | solution.py:37
  62.4 1.2 %copy.43 = f32[512,192]{0,1:T(8,128)S(1)} copy(f32[512,192]{1,0:T(8,128)} %gather_fusion.11) | data formatting | bytes 786432 | tf_op jit(solution)/shard_map/jit(_take)/gather | solution.py:34
  65.9 1.9 %collective-permute-start.6 = (f32[128,192]{0,1:T(8,128)S(1)}, f32[128,192]{0,1:T(8,128)S(1)}, u32[]{:S(2)}, u32[]{:S(2)}) collective-permute-start(f32[128,192]{0,1:T(8,128)S(1)} %get-tuple-element.16), channel_id=1, source_target_pairs={{0,4},{4,8},{8,12},{12,16},{16,20},{20,24},{24,28},{28,32},{32,36}... | collective-permute-start | bytes 294920 | tf_op jit(solution)/shard_map/ppermute | solution.py:18
  67.8 5.8 %collective-permute-start.7 = (f32[128,192]{0,1:T(8,128)S(1)}, f32[128,192]{0,1:T(8,128)S(1)}, u32[]{:S(2)}, u32[]{:S(2)}) collective-permute-start(f32[128,192]{0,1:T(8,128)S(1)} %get-tuple-element.17), channel_id=1, source_target_pairs={{4,0},{8,4},{12,8},{16,12},{20,16},{24,20},{28,24},{32,28},{36,32}... | collective-permute-start | bytes 294920 | tf_op jit(solution)/shard_map/ppermute | solution.py:19
  74.0 1.8 %collective-permute-done.7 = f32[128,192]{0,1:T(8,128)S(1)} collective-permute-done((f32[128,192]{0,1:T(8,128)S(1)}, f32[128,192]{0,1:T(8,128)S(1)}, u32[]{:S(2)}, u32[]{:S(2)}) %collective-permute-start.7) | collective-permute-done | bytes 98336 | tf_op jit(solution)/shard_map/ppermute | solution.py:19
  76.2 1.6 %gather_fusion.16 = f32[512,192]{1,0:T(8,128)S(1)} fusion(f32[776,192]{1,0:T(8,128)S(1)} %copy.52, s32[1024]{0:T(1024)S(1)} %pad_clamp_fusion.3), kind=kCustom, calls=%fused_computation.16.clone | custom fusion | bytes 788480 | tf_op jit(solution)/shard_map/jit(_take)/gather | solution.py:34
  77.8 1.6 %gather_fusion.17 = f32[512,192]{1,0:T(8,128)S(1)} fusion(f32[776,192]{1,0:T(8,128)S(1)} %copy.52, s32[1024]{0:T(1024)S(1)} %pad_clamp_fusion.2), kind=kCustom, calls=%fused_computation.17.clone | custom fusion | bytes 788480 | tf_op jit(solution)/shard_map/jit(_take)/gather | solution.py:35
  79.3 1.6 %gather_fusion.18 = f32[512,192]{1,0:T(8,128)S(1)} fusion(f32[776,192]{1,0:T(8,128)S(1)} %copy.52, s32[1024]{0:T(1024)S(1)} %pad_clamp_fusion.1), kind=kCustom, calls=%fused_computation.18.clone | custom fusion | bytes 788480 | tf_op jit(solution)/shard_map/jit(_take)/gather | solution.py:36
  80.9 1.6 %gather_fusion.19 = f32[512,192]{1,0:T(8,128)S(1)} fusion(f32[776,192]{1,0:T(8,128)S(1)} %copy.52, s32[1024]{0:T(1024)S(1)} %pad_clamp_fusion), kind=kCustom, calls=%fused_computation.19.clone | custom fusion | bytes 788480 | tf_op jit(solution)/shard_map/jit(_take)/gather | solution.py:37
  83.3 1.0 copy_bitcast_fusion.1
  84.3 4.5 %all-to-all-start = ((f32[192,4,128]{2,0,1:T(8,128)}), f32[192,4,128]{2,0,1:T(8,128)S(1)}, u32[]{:S(2)}, u32[]{:S(2)}) async-start(f32[192,4,128]{2,0,1:T(8,128)} %copy_bitcast_fusion.1), calls=%async_computation | async-start | bytes 786432 | tf_op jit(solution)/shard_map/all_to_all | solution.py:123
  88.8 7.3 %all-to-all-done = f32[192,4,128]{2,0,1:T(8,128)S(1)} async-done(((f32[192,4,128]{2,0,1:T(8,128)}), f32[192,4,128]{2,0,1:T(8,128)S(1)}, u32[]{:S(2)}, u32[]{:S(2)}) %all-to-all-start) | async-done | bytes 393248 | tf_op jit(solution)/shard_map/all_to_all | solution.py:123
  96.9 9.8 %all_to_all.30 = f32[768,1,128]{2,1,0:T(1,128)S(1)} all-to-all(f32[768,1,128]{2,1,0:T(1,128)S(1)} %bitcast.34), channel_id=1, replica_groups=mesh['tiles'=64,'comp'=4] {'comp'}, dimensions={0} | all-to-all | bytes 786432 | tf_op jit(solution)/shard_map/all_to_all | solution.py:139
  (111 shorter events, 19.1 us)
Async XLA Ops:
  0.0 0.8 copy-start.4
  0.0 0.8 copy-start.3
  3.2 9.4 %copy-start.1 = (s32[4,512]{1,0:T(4,128)S(1)}, s32[4,512]{1,0:T(4,128)}, u32[]{:S(2)}) copy-start(s32[4,512]{1,0:T(4,128)} %param.20) | copy-start | bytes 24580
  3.2 13.1 %collective-permute-start = (f32[128,192]{0,1:T(8,128)S(1)}, f32[128,192]{0,1:T(8,128)S(1)}, u32[]{:S(2)}, u32[]{:S(2)}) collective-permute-start(f32[128,192]{0,1:T(8,128)S(1)} %get-tuple-element.22), channel_id=1, source_target_pairs={{0,4},{4,8},{8,12},{12,16},{16,20},{20,24},{24,28},{28,32},{32,36}... | collective-permute-start | bytes 294920 | tf_op jit(solution)/shard_map/ppermute | solution.py:18
  5.1 11.2 %collective-permute-start.1 = (f32[128,192]{0,1:T(8,128)S(1)}, f32[128,192]{0,1:T(8,128)S(1)}, u32[]{:S(2)}, u32[]{:S(2)}) collective-permute-start(f32[128,192]{0,1:T(8,128)S(1)} %get-tuple-element.23), channel_id=1, source_target_pairs={{4,0},{8,4},{12,8},{16,12},{20,16},{24,20},{28,24},{32,28},{36,32}... | collective-permute-start | bytes 294920 | tf_op jit(solution)/shard_map/ppermute | solution.py:19
  12.8 0.7 copy-start.2
  15.5 0.7 copy-start.5
  15.5 0.7 copy-start.6
  23.5 1.0 copy-start
  26.2 8.0 %collective-permute-start.2 = (f32[128,192]{0,1:T(8,128)S(1)}, f32[128,192]{0,1:T(8,128)S(1)}, u32[]{:S(2)}, u32[]{:S(2)}) collective-permute-start(f32[128,192]{0,1:T(8,128)S(1)} %get-tuple-element.20), channel_id=1, source_target_pairs={{0,4},{4,8},{8,12},{12,16},{16,20},{20,24},{24,28},{28,32},{32,36}... | collective-permute-start | bytes 294920 | tf_op jit(solution)/shard_map/ppermute | solution.py:18
  28.1 8.0 %collective-permute-start.3 = (f32[128,192]{0,1:T(8,128)S(1)}, f32[128,192]{0,1:T(8,128)S(1)}, u32[]{:S(2)}, u32[]{:S(2)}) collective-permute-start(f32[128,192]{0,1:T(8,128)S(1)} %get-tuple-element.21), channel_id=1, source_target_pairs={{4,0},{8,4},{12,8},{16,12},{20,16},{24,20},{28,24},{32,28},{36,32}... | collective-permute-start | bytes 294920 | tf_op jit(solution)/shard_map/ppermute | solution.py:19
  45.2 8.1 %collective-permute-start.4 = (f32[128,192]{0,1:T(8,128)S(1)}, f32[128,192]{0,1:T(8,128)S(1)}, u32[]{:S(2)}, u32[]{:S(2)}) collective-permute-start(f32[128,192]{0,1:T(8,128)S(1)} %get-tuple-element.18), channel_id=1, source_target_pairs={{0,4},{4,8},{8,12},{12,16},{16,20},{20,24},{24,28},{28,32},{32,36}... | collective-permute-start | bytes 294920 | tf_op jit(solution)/shard_map/ppermute | solution.py:18
  47.1 8.0 %collective-permute-start.5 = (f32[128,192]{0,1:T(8,128)S(1)}, f32[128,192]{0,1:T(8,128)S(1)}, u32[]{:S(2)}, u32[]{:S(2)}) collective-permute-start(f32[128,192]{0,1:T(8,128)S(1)} %get-tuple-element.19), channel_id=1, source_target_pairs={{4,0},{8,4},{12,8},{16,12},{20,16},{24,20},{28,24},{32,28},{36,32}... | collective-permute-start | bytes 294920 | tf_op jit(solution)/shard_map/ppermute | solution.py:19
  65.9 8.1 %collective-permute-start.6 = (f32[128,192]{0,1:T(8,128)S(1)}, f32[128,192]{0,1:T(8,128)S(1)}, u32[]{:S(2)}, u32[]{:S(2)}) collective-permute-start(f32[128,192]{0,1:T(8,128)S(1)} %get-tuple-element.16), channel_id=1, source_target_pairs={{0,4},{4,8},{8,12},{12,16},{16,20},{20,24},{24,28},{28,32},{32,36}... | collective-permute-start | bytes 294920 | tf_op jit(solution)/shard_map/ppermute | solution.py:18
  67.8 8.0 %collective-permute-start.7 = (f32[128,192]{0,1:T(8,128)S(1)}, f32[128,192]{0,1:T(8,128)S(1)}, u32[]{:S(2)}, u32[]{:S(2)}) collective-permute-start(f32[128,192]{0,1:T(8,128)S(1)} %get-tuple-element.17), channel_id=1, source_target_pairs={{4,0},{8,4},{12,8},{16,12},{20,16},{24,20},{28,24},{32,28},{36,32}... | collective-permute-start | bytes 294920 | tf_op jit(solution)/shard_map/ppermute | solution.py:19
  84.3 11.8 %all-to-all-start = ((f32[192,4,128]{2,0,1:T(8,128)}), f32[192,4,128]{2,0,1:T(8,128)S(1)}, u32[]{:S(2)}, u32[]{:S(2)}) async-start(f32[192,4,128]{2,0,1:T(8,128)} %copy_bitcast_fusion.1), calls=%async_computation | async-start | bytes 786432 | tf_op jit(solution)/shard_map/all_to_all | solution.py:123
where the time goes:
time: 108 us
  local copies, waits for them, and re-layouts  41.1 us (38%)
  starting transfers between devices  37.2 us (34%)
  waiting for transfers between devices  13.6 us (13%)
  blocking collectives  9.77 us (9%)
  other arithmetic  5.25 us (5%)
    ppermute x4, starting transfers between devices, extended_2(): after = lax.ppermute(first, axis, down)  25.1 us
    all_to_all x1, blocking collectives, shards(): lax.all_to_all(result.reshape(comps, 1, quarter), 'comp', split_axis=0, c...  9.77 us
    gather x8, local copies, waits for them, and re-layouts, advect_rows(): from_west = jnp.take(extended, neighbours[0], axis=0)  8.71 us
    ppermute x4, starting transfers between devices, extended_2(): before = lax.ppermute(last, axis, up)  7.68 us
    all_to_all x1, waiting for transfers between devices, shards(): lax.all_to_all(by_owner, 'comp', split_axis=1, concat_axis=0, tiled=True)  7.3 us
    gather x8, local copies, waits for them, and re-layouts, advect_rows(): from_south = jnp.take(extended, neighbours[2], axis=0)  7.01 us
    gather x8, local copies, waits for them, and re-layouts, advect_rows(): from_north = jnp.take(extended, neighbours[3], axis=0)  7.01 us
    gather x8, local copies, waits for them, and re-layouts, advect_rows(): from_east = jnp.take(extended, neighbours[1], axis=0)  7 us
  transfers between devices with their start and end apart: 9, of which 7 were waited for; matrix products, arithmetic and copies ran while one was open for 2% of the time, Pallas kernels for 0%

commit v1 on v0

v1 whole, which is shorter than its diff:
```python
import math

import jax
import jax.numpy as jnp
import numpy as np
from jax import lax
from jax.experimental import pallas as pl
from jax.experimental.pallas import tpu as pltpu
from jax.sharding import PartitionSpec as P

NSUB = 4
NTH = 24
NK = 32
PTS = 512
RIM = 128
EXT = PTS + 2 * RIM
COMP_AXIS = 4
DIRS = NTH // COMP_AXIS
ROWS = DIRS * NK
COMPS = NTH * NK
OWN_N = 2 * PTS
SEND_N = 4 * RIM
GROUPS = ((0, 3), (3, 6))
MESH = pl.DeviceIdType.MESH
STEP = np.float32(2.0 * math.pi / NTH)
LOG_RATIO = np.float32(math.log(1.1))


def pick(index, values):
    chosen = jnp.float32(values[0])
    for place in range(1, len(values)):
        chosen = jnp.where(index == place, jnp.float32(values[place]), chosen)
    return chosen


def halves(values):
    high = values.astype(jnp.bfloat16)
    low = (values - high.astype(jnp.float32)).astype(jnp.bfloat16)
    return jnp.concatenate([high, low], axis=0)


def gathered(split, table):
    both = jnp.dot(split, table, preferred_element_type=jnp.float32)
    rows = both.shape[0] // 2
    return both[:rows] + both[rows:]


def wide(column, lanes):
    return jnp.concatenate([column] * (lanes // RIM), axis=1)


def onehot(first, count, index):
    places = lax.broadcasted_iota(jnp.int32, (count, index.shape[1]), 0) + first
    return jnp.where(places == index, 1.0, 0.0).astype(jnp.bfloat16)


def kernel(
    action_hbm,
    speed_hbm,
    turning_hbm,
    shift_hbm,
    wind_hbm,
    dir_hbm,
    mask_hbm,
    links_hbm,
    rows_hbm,
    out_ref,
    spec,
    speed,
    turning,
    shift,
    wind,
    wdir,
    mask,
    links,
    rows,
    table,
    send_table,
    across,
    along,
    keep,
    outgoing,
    rim,
    pending,
    pending_send,
    gain,
    ghost,
    part,
    parts,
    load_sem,
    halo_send,
    halo_recv,
    ghost_send,
    ghost_recv,
    part_send,
    part_recv,
):
    tile = lax.axis_index("tiles")
    comp = lax.axis_index("comp")
    tiles = lax.axis_size("tiles")
    before_tile = lax.rem(tile + tiles - 1, tiles)
    after_tile = lax.rem(tile + 1, tiles)
    comp_at = [lax.rem(comp + step, COMP_AXIS) for step in range(COMP_AXIS)]

    barrier = pltpu.get_barrier_semaphore()
    for place in (
        (before_tile, comp),
        (after_tile, comp),
        (tile, comp_at[1]),
        (tile, comp_at[2]),
        (tile, comp_at[3]),
    ):
        pl.semaphore_signal(barrier, inc=1, device_id=place, device_id_type=MESH)

    loads = [
        pltpu.make_async_copy(source, target, load_sem.at[number])
        for number, (source, target) in enumerate(
            (
                (rows_hbm, rows),
                (mask_hbm, mask),
                (action_hbm, spec),
                (links_hbm, links),
                (speed_hbm, speed),
                (turning_hbm, turning),
                (shift_hbm, shift),
                (wind_hbm, wind),
                (dir_hbm, wdir),
            )
        )
    ]
    for load in loads:
        load.start()

    def halo_copies(step, group):
        first, last = (GROUPS[group][0] * NK, GROUPS[group][1] * NK)
        span = pl.ds(first, last - first)
        copies = []
        for side, target in ((0, before_tile), (1, after_tile)):
            copies.append(
                pltpu.make_async_remote_copy(
                    src_ref=outgoing.at[step, side, span],
                    dst_ref=rim.at[step, 1 - side, span],
                    send_sem=halo_send.at[step, group, side],
                    recv_sem=halo_recv.at[step, group, 1 - side],
                    device_id=(target, comp),
                    device_id_type=MESH,
                )
            )
        return copies

    started = []

    def send_halo(step, group, values):
        first, last = (GROUPS[group][0] * NK, GROUPS[group][1] * NK)
        outgoing[step, 0, first:last] = values[:, :RIM]
        outgoing[step, 1, first:last] = values[:, RIM:]
        for copy in halo_copies(step, group):
            copy.start()
            started.append(copy)

    loads[0].wait()
    send_table[...] = onehot(0, PTS, rows[...])
    loads[1].wait()
    wet = mask[...].astype(jnp.float32)
    loads[2].wait()
    spec[...] = spec[...] * wet
    splits = []
    first_sends = []
    for first, last in GROUPS:
        split = halves(spec[first * NK : last * NK])
        splits.append(split)
        first_sends.append(gathered(split, send_table[...]))
    pl.semaphore_wait(barrier, 5)
    for group in range(len(GROUPS)):
        send_halo(0, group, first_sends[group])

    loads[4].wait()
    diagonal = lax.broadcasted_iota(jnp.int32, (NK, NK), 0) == lax.broadcasted_iota(
        jnp.int32, (NK, NK), 1
    )
    courant = jnp.sum(jnp.where(diagonal, speed[...], 0.0), axis=1, keepdims=True)
    courant = jnp.broadcast_to(courant, (NK, RIM))
    angles = np.arange(NTH).astype(np.float32) * STEP
    cosines = np.abs(np.cos(angles)).reshape(COMP_AXIS, DIRS)
    sines = np.abs(np.sin(angles)).reshape(COMP_AXIS, DIRS)
    for d in range(DIRS):
        span = slice(d * NK, (d + 1) * NK)
        speed_x = courant * pick(comp, cosines[:, d])
        speed_y = courant * pick(comp, sines[:, d])
        across[span] = speed_x
        along[span] = speed_y
        keep[span] = 1.0 - speed_x - speed_y

    loads[3].wait()
    west_side = jnp.logical_or(comp == 0, comp == COMP_AXIS - 1)
    south_side = comp < 2
    for axis, index in enumerate(
        (
            jnp.where(west_side, links[0:1], links[1:2]),
            jnp.where(south_side, links[2:3], links[3:4]),
        )
    ):
        no_left = jnp.logical_and(tile == 0, index < RIM)
        no_right = jnp.logical_and(tile == tiles - 1, index >= RIM + PTS)
        nothing = jnp.logical_or(jnp.logical_or(no_left, no_right), mask[...] == 0)
        index = jnp.where(nothing, EXT, index)
        lanes = pl.ds(axis * PTS, PTS)
        table[0:PTS, lanes] = onehot(RIM, PTS, index)
        table[PTS : PTS + RIM, lanes] = onehot(0, RIM, index)
        table[PTS + RIM : EXT, lanes] = onehot(RIM + PTS, RIM, index)
    for axis in range(2):
        picked = jnp.dot(
            table[:, axis * PTS : (axis + 1) * PTS],
            send_table[...],
            preferred_element_type=jnp.float32,
        )
        first = OWN_N + axis * 2 * RIM
        table[:, first : first + 2 * RIM] = picked.astype(jnp.bfloat16)

    def own_part(group, split, values, sends, with_sends):
        first, last = (GROUPS[group][0] * NK, GROUPS[group][1] * NK)
        span = slice(first, last)
        picked = gathered(split, table[0:PTS, 0:OWN_N])
        pending[span] = (
            wide(keep[span], PTS) * values
            + wide(across[span], PTS) * picked[:, :PTS]
            + wide(along[span], PTS) * picked[:, PTS:]
        )
        if with_sends:
            picked = gathered(split, table[0:PTS, OWN_N:])
            pending_send[span] = (
                wide(keep[span], 2 * RIM) * sends
                + wide(across[span], 2 * RIM) * picked[:, : 2 * RIM]
                + wide(along[span], 2 * RIM) * picked[:, 2 * RIM :]
            )

    for group, (first, last) in enumerate(GROUPS):
        own_part(group, splits[group], spec[first * NK : last * NK], first_sends[group], True)

    for number in (5, 6, 7, 8):
        loads[number].wait()
    sigma = jnp.exp(
        (lax.broadcasted_iota(jnp.int32, (NK, RIM), 0) - NK // 2).astype(jnp.float32) * LOG_RATIO
    )
    sigma = wide(sigma, PTS)
    angle = (lax.broadcasted_iota(jnp.int32, (8, PTS), 0) + comp * DIRS).astype(jnp.float32) * STEP
    aligned = jnp.cos(angle - wdir[...])
    driven = wind[...] * sigma
    for d in range(DIRS):
        grown = 0.4 * jnp.maximum(driven * aligned[d : d + 1] - 0.3, 0.0)
        gain[d * NK : (d + 1) * NK] = wet * (1.0 + grown)

    ghost_copies = [
        pltpu.make_async_remote_copy(
            src_ref=spec.at[pl.ds(at * NK, NK)],
            dst_ref=ghost.at[slot],
            send_sem=ghost_send.at[slot],
            recv_sem=ghost_recv.at[slot],
            device_id=(tile, target),
            device_id_type=MESH,
        )
        for slot, at, target in ((0, DIRS - 1, comp_at[1]), (1, 0, comp_at[3]))
    ]

    for step in range(NSUB):
        for group, (low, high) in enumerate(GROUPS):
            first, last = (low * NK, high * NK)
            span = slice(first, last)
            for copy in halo_copies(step, group):
                copy.wait_recv()
            split = halves(jnp.concatenate([rim[step, 0, span], rim[step, 1, span]], axis=1))
            if step < NSUB - 1:
                picked = gathered(split, table[PTS:EXT, OWN_N:])
                sends = (
                    pending_send[span]
                    + wide(across[span], 2 * RIM) * picked[:, : 2 * RIM]
                    + wide(along[span], 2 * RIM) * picked[:, 2 * RIM :]
                )
                send_halo(step + 1, group, sends)
            picked = gathered(split, table[PTS:EXT, 0:OWN_N])
            values = (
                pending[span]
                + wide(across[span], PTS) * picked[:, :PTS]
                + wide(along[span], PTS) * picked[:, PTS:]
            )
            if step < NSUB - 1:
                own_part(group, halves(values), values, sends, step < NSUB - 2)
            else:
                spec[span] = values
                if low == 0:
                    ghost_copies[1].start()
                if high == DIRS:
                    ghost_copies[0].start()

    turn = turning[...]
    moved = shift[...]
    freq = lax.broadcasted_iota(jnp.int32, (NK, PTS), 0)

    def shifted(values):
        lower = jnp.where(freq == 0, 0.0, pltpu.roll(values, 1, 0))
        upper = jnp.where(freq == NK - 1, 0.0, pltpu.roll(values, NK - 1, 0))
        return values - jnp.abs(moved) * (values - jnp.where(moved > 0, lower, upper))

    total = spec[0:NK]
    for d in range(1, DIRS):
        total = total + spec[d * NK : (d + 1) * NK]
    total = shifted(total) * sigma
    energy = jnp.sum(total, axis=0, keepdims=True)
    moment = jnp.sum(total * sigma, axis=0, keepdims=True)
    part[0:1] = energy
    part[1:2] = moment
    part_copies = [
        pltpu.make_async_remote_copy(
            src_ref=part,
            dst_ref=parts.at[hop - 1],
            send_sem=part_send.at[hop - 1],
            recv_sem=part_recv.at[hop - 1],
            device_id=(tile, comp_at[hop]),
            device_id_type=MESH,
        )
        for hop in (2, 1, 3)
    ]
    for copy in part_copies:
        copy.start()

    def refracted(d):
        values = spec[d * NK : (d + 1) * NK]
        before = ghost[0] if d == 0 else spec[(d - 1) * NK : d * NK]
        beyond = ghost[1] if d == DIRS - 1 else spec[(d + 1) * NK : (d + 2) * NK]
        return values - jnp.abs(turn) * (values - jnp.where(turn > 0, before, beyond))

    def grow(d):
        span = slice(d * NK, (d + 1) * NK)
        gain[span] = gain[span] * shifted(refracted(d))

    for d in range(1, DIRS - 1):
        grow(d)
    ghost_copies[0].wait_recv()
    grow(0)
    ghost_copies[1].wait_recv()
    grow(DIRS - 1)
    for copy in part_copies:
        copy.wait_recv()
    whole = (part[...] + parts[0] + parts[1] + parts[2]) * jnp.float32(1.0 / COMPS)
    energy = whole[0:1]
    mean_freq = whole[1:2] / jnp.maximum(energy, 0.05)
    strength = mean_freq * mean_freq * mean_freq * energy * energy
    damping = 0.005 * (sigma * sigma) * strength
    factor = 1.0 / (1.0 + damping)
    for d in range(DIRS):
        span = slice(d * NK, (d + 1) * NK)
        out_ref[span] = gain[span] * factor

    for copy in started + ghost_copies + part_copies:
        copy.wait_send()


def shards(
    action,
    speed_courant,
    turning,
    freq_shift,
    wind_speed,
    wind_dir,
    sea_mask,
    neighbours,
    halo_rows,
):
    vmem = pltpu.VMEM
    f32 = jnp.float32
    dma = pltpu.SemaphoreType.DMA
    groups = len(GROUPS)

    def row(values):
        return values.reshape(1, values.shape[0])

    return pl.pallas_call(
        kernel,
        out_shape=jax.ShapeDtypeStruct((ROWS, PTS), f32),
        in_specs=[pl.BlockSpec(memory_space=pl.ANY)] * 9,
        out_specs=pl.BlockSpec(memory_space=pltpu.VMEM),
        scratch_shapes=[
            vmem((ROWS, PTS), f32),
            vmem((1, NK), f32),
            vmem((1, PTS), f32),
            vmem((1, PTS), f32),
            vmem((1, PTS), f32),
            vmem((1, PTS), f32),
            vmem((1, PTS), jnp.int32),
            vmem((4, PTS), jnp.int32),
            vmem((1, 2 * RIM), jnp.int32),
            vmem((EXT, OWN_N + SEND_N), jnp.bfloat16),
            vmem((PTS, 2 * RIM), jnp.bfloat16),
            vmem((ROWS, RIM), f32),
            vmem((ROWS, RIM), f32),
            vmem((ROWS, RIM), f32),
            vmem((NSUB, 2, ROWS, RIM), f32),
            vmem((NSUB, 2, ROWS, RIM), f32),
            vmem((ROWS, PTS), f32),
            vmem((ROWS, 2 * RIM), f32),
            vmem((ROWS, PTS), f32),
            vmem((2, NK, PTS), f32),
            vmem((2, PTS), f32),
            vmem((3, 2, PTS), f32),
            dma((9,)),
            dma((NSUB, groups, 2)),
            dma((NSUB, groups, 2)),
            dma((2,)),
            dma((2,)),
            dma((3,)),
            dma((3,)),
        ],
        compiler_params=pltpu.CompilerParams(
            collective_id=0, has_side_effects=True, vmem_limit_bytes=48 * 1024 * 1024
        ),
        name="wave_step",
    )(
        action,
        row(speed_courant),
        row(turning),
        row(freq_shift),
        row(wind_speed),
        row(wind_dir),
        row(sea_mask),
        neighbours,
        row(halo_rows),
    )


def solution(mesh):
    placed = (
        P("comp", "tiles"),
        P(),
        P("tiles"),
        P("tiles"),
        P("tiles"),
        P("tiles"),
        P("tiles"),
        P(None, "tiles"),
        P("tiles"),
    )
    return jax.shard_map(
        shards, mesh=mesh, in_specs=placed, out_specs=P("comp", "tiles"), check_vma=False
    )
```

time: 108 us -> 37.5 us (0.35)
  the two profiles are of different devices: /device:TPU:6 before, /device:TPU:8 now
where the time goes in v1:
time: 37.5 us; the launch traced here: 37.3 us
  Pallas kernels  32.1 us (86%)
  local copies, waits for them, and re-layouts  5.15 us (14%)
    pallas_call x1, Pallas kernels, shards(): pl.pallas_call(kernel, out_shape=jax.ShapeDtypeStruct((ROWS, PTS), f32),...  32.1 us
    unnamed x19, local copies, waits for them, and re-layouts  5.15 us

profile of v1, /device:TPU:8, one launch (start us, length us, event | category | flops | bytes accessed | tf_op | source)
XLA Modules:
  0.0 37.3 jit_solution(15672060479735233827)
XLA Ops:
  0.0 0.0 copy-start.1
  0.0 0.0 copy-start.3
  0.0 0.0 copy-start.2
  0.0 0.0 copy-start.7
  0.0 0.7 %copy-done.1 = s32[4,512]{1,0:T(4,128)S(1)} copy-done((s32[4,512]{1,0:T(4,128)S(1)}, s32[4,512]{1,0:T(4,128)}, u32[]{:S(2)}) %copy-start.1) | copy-done | bytes 8216
  0.7 0.0 copy-done.3
  0.7 0.0 copy-done.2
  0.7 0.0 copy-done.7
  0.7 0.0 copy-start
  0.7 1.0 %copy-done = f32[192,512]{1,0:T(8,128)S(1)} copy-done((f32[192,512]{1,0:T(8,128)S(1)}, f32[192,512]{1,0:T(8,128)}, u32[]{:S(2)}) %copy-start) | copy-done | bytes 393240
  1.7 0.0 copy-start.4
  1.7 0.7 %copy-done.4 = f32[512]{0:T(512)S(1)} copy-done((f32[512]{0:T(512)S(1)}, f32[512]{0:T(512)}, u32[]{:S(2)}) %copy-start.4) | copy-done | bytes 2072
  2.4 0.0 copy-start.5
  2.4 0.7 %copy-done.5 = f32[512]{0:T(512)S(1)} copy-done((f32[512]{0:T(512)S(1)}, f32[512]{0:T(512)}, u32[]{:S(2)}) %copy-start.5) | copy-done | bytes 2072
  3.1 0.0 copy-start.6
  3.1 0.7 %copy-done.6 = s32[512]{0:T(512)S(1)} copy-done((s32[512]{0:T(512)S(1)}, s32[512]{0:T(512)}, u32[]{:S(2)}) %copy-start.6) | copy-done | bytes 2072
  3.8 0.0 copy-start.8
  3.8 0.7 %copy-done.8 = f32[32]{0:T(128)S(1)} copy-done((f32[32]{0:T(128)S(1)}, f32[32]{0:T(128)}, u32[]{:S(2)}) %copy-start.8) | copy-done | bytes 152
  4.4 32.1 %wave_step.1 = f32[192,512]{1,0:T(8,128)S(1)} custom-call(f32[192,512]{1,0:T(8,128)S(1)} %copy-done, f32[1,32]{1,0:T(1,128)S(1)} %bitcast.13, f32[1,512]{1,0:T(1,128)S(1)} %bitcast.7, f32[1,512]{1,0:T(1,128)S(1)} %bitcast.8, f32[1,512]{1,0:T(1,128)S(1)} %bitcast.9, f32[1,512]{1,0:T(1,128)S(1)} %bitcast.10, s32[1,512]{1,0:T(1,128)S(1)} %bitcast.11, ...), custom_call_target="tpu_custom_call" | custom-call | tf_op jit(solution)/shard_map/wave_step/pallas_call | solution.py:377
  36.5 0.7 %copy.11 = f32[192,512]{1,0:T(8,128)} copy(f32[192,512]{1,0:T(8,128)S(1)} %wave_step.1) | data formatting | bytes 786432
Async XLA Ops:
  0.0 0.7 %copy-start.1 = (s32[4,512]{1,0:T(4,128)S(1)}, s32[4,512]{1,0:T(4,128)}, u32[]{:S(2)}) copy-start(s32[4,512]{1,0:T(4,128)} %links_hbm.1) | copy-start | bytes 24580
  0.0 0.7 %copy-start.3 = (f32[512]{0:T(512)S(1)}, f32[512]{0:T(512)}, u32[]{:S(2)}) copy-start(f32[512]{0:T(512)} %param.12) | copy-start | bytes 6148
  0.0 0.7 %copy-start.2 = (f32[512]{0:T(512)S(1)}, f32[512]{0:T(512)}, u32[]{:S(2)}) copy-start(f32[512]{0:T(512)} %param.11) | copy-start | bytes 6148
  0.0 0.7 %copy-start.7 = (s32[256]{0:T(256)S(1)}, s32[256]{0:T(256)}, u32[]{:S(2)}) copy-start(s32[256]{0:T(256)} %param.17) | copy-start | bytes 3076
  0.7 1.0 %copy-start = (f32[192,512]{1,0:T(8,128)S(1)}, f32[192,512]{1,0:T(8,128)}, u32[]{:S(2)}) copy-start(f32[192,512]{1,0:T(8,128)} %action_hbm.1) | copy-start | bytes 1179652
  1.7 0.7 %copy-start.4 = (f32[512]{0:T(512)S(1)}, f32[512]{0:T(512)}, u32[]{:S(2)}) copy-start(f32[512]{0:T(512)} %param.13) | copy-start | bytes 6148
  2.4 0.7 %copy-start.5 = (f32[512]{0:T(512)S(1)}, f32[512]{0:T(512)}, u32[]{:S(2)}) copy-start(f32[512]{0:T(512)} %param.14) | copy-start | bytes 6148
  3.1 0.7 %copy-start.6 = (s32[512]{0:T(512)S(1)}, s32[512]{0:T(512)}, u32[]{:S(2)}) copy-start(s32[512]{0:T(512)} %param.15) | copy-start | bytes 6148
  3.8 0.7 %copy-start.8 = (f32[32]{0:T(128)S(1)}, f32[32]{0:T(128)}, u32[]{:S(2)}) copy-start(f32[32]{0:T(128)} %param.10) | copy-start | bytes 388

commit v2 on v1

--- a/solution.py
+++ b/solution.py
@@ -20,6 +20,7 @@
 COMPS = NTH * NK
 OWN_N = 2 * PTS
 SEND_N = 4 * RIM
+NEAR, FAR = 0, 1
 GROUPS = ((0, 3), (3, 6))
 MESH = pl.DeviceIdType.MESH
 STEP = np.float32(2.0 * math.pi / NTH)
@@ -76,6 +77,7 @@
     rows,
     table,
     send_table,
+    far_table,
     across,
     along,
     keep,
@@ -83,10 +85,13 @@
     rim,
     pending,
     pending_send,
+    mended,
     gain,
     ghost,
     part,
     parts,
+    spots,
+    far_spots,
     load_sem,
     halo_send,
     halo_recv,
@@ -94,23 +99,31 @@
     ghost_recv,
     part_send,
     part_recv,
+    spot_send,
+    spot_recv,
 ):
     tile = lax.axis_index("tiles")
     comp = lax.axis_index("comp")
     tiles = lax.axis_size("tiles")
-    before_tile = lax.rem(tile + tiles - 1, tiles)
-    after_tile = lax.rem(tile + 1, tiles)
+    first_core = lax.rem(tile, 2) == 0
+    near_tile = jnp.where(first_core, tile + 1, tile - 1)
+    far_tile = jnp.where(first_core, tile - 1, tile + 1)
+    has_far = jnp.logical_and(far_tile >= 0, far_tile < tiles)
+    far_tile = jnp.clip(far_tile, 0, tiles - 1)
     comp_at = [lax.rem(comp + step, COMP_AXIS) for step in range(COMP_AXIS)]
 
     barrier = pltpu.get_barrier_semaphore()
     for place in (
-        (before_tile, comp),
-        (after_tile, comp),
+        (near_tile, comp),
         (tile, comp_at[1]),
         (tile, comp_at[2]),
         (tile, comp_at[3]),
     ):
         pl.semaphore_signal(barrier, inc=1, device_id=place, device_id_type=MESH)
+
+    @pl.when(has_far)
+    def _():
+        pl.semaphore_signal(barrier, inc=1, device_id=(far_tile, comp), device_id_type=MESH)
 
     loads = [
         pltpu.make_async_copy(source, target, load_sem.at[number])
@@ -131,48 +144,103 @@
     for load in loads:
         load.start()
 
-    def halo_copies(step, group):
+    def span_of(group):
+        return slice(GROUPS[group][0] * NK, GROUPS[group][1] * NK)
+
+    def halo_copy(level, side, group):
         first, last = (GROUPS[group][0] * NK, GROUPS[group][1] * NK)
         span = pl.ds(first, last - first)
-        copies = []
-        for side, target in ((0, before_tile), (1, after_tile)):
-            copies.append(
-                pltpu.make_async_remote_copy(
-                    src_ref=outgoing.at[step, side, span],
-                    dst_ref=rim.at[step, 1 - side, span],
-                    send_sem=halo_send.at[step, group, side],
-                    recv_sem=halo_recv.at[step, group, 1 - side],
-                    device_id=(target, comp),
-                    device_id_type=MESH,
-                )
-            )
-        return copies
-
-    started = []
-
-    def send_halo(step, group, values):
-        first, last = (GROUPS[group][0] * NK, GROUPS[group][1] * NK)
-        outgoing[step, 0, first:last] = values[:, :RIM]
-        outgoing[step, 1, first:last] = values[:, RIM:]
-        for copy in halo_copies(step, group):
-            copy.start()
-            started.append(copy)
+        return pltpu.make_async_remote_copy(
+            src_ref=outgoing.at[level, side, span],
+            dst_ref=rim.at[level, side, span],
+            send_sem=halo_send.at[level, side, group],
+            recv_sem=halo_recv.at[level, side, group],
+            device_id=(near_tile if side == NEAR else far_tile, comp),
+            device_id_type=MESH,
+        )
+
+    def only_if_far(side, action):
+        if side == NEAR:
+            action()
+        else:
+            pl.when(has_far)(action)
+
+    def send_halo(level, side, group, values):
+        outgoing[level, side, span_of(group)] = values
+        only_if_far(side, lambda: halo_copy(level, side, group).start())
+
+    def await_halo(level, side, group):
+        only_if_far(side, lambda: halo_copy(level, side, group).wait_recv())
 
     loads[0].wait()
-    send_table[...] = onehot(0, PTS, rows[...])
+    low_rows, high_rows = (rows[:, 0:RIM], rows[:, RIM : 2 * RIM])
+    near_rows = jnp.where(first_core, high_rows, low_rows)
+    far_rows = jnp.where(first_core, low_rows, high_rows)
+    picker = onehot(0, PTS, jnp.concatenate([near_rows, far_rows], axis=1))
     loads[1].wait()
     wet = mask[...].astype(jnp.float32)
     loads[2].wait()
     spec[...] = spec[...] * wet
     splits = []
     first_sends = []
-    for first, last in GROUPS:
-        split = halves(spec[first * NK : last * NK])
+    for group in range(len(GROUPS)):
+        split = halves(spec[span_of(group)])
         splits.append(split)
-        first_sends.append(gathered(split, send_table[...]))
-    pl.semaphore_wait(barrier, 5)
+        first_sends.append(gathered(split, picker))
+
+    @pl.when(jnp.logical_not(has_far))
+    def _():
+        for level in range(NSUB):
+            rim[level, FAR] = jnp.zeros((ROWS, RIM), jnp.float32)
+        far_spots[...] = jnp.full((1, 2 * RIM), float(RIM), jnp.float32)
+
+    pl.semaphore_wait(barrier, jnp.where(has_far, 5, 4))
+
     for group in range(len(GROUPS)):
-        send_halo(0, group, first_sends[group])
+        send_halo(0, FAR, group, first_sends[group][:, RIM:])
+        send_halo(0, NEAR, group, first_sends[group][:, :RIM])
+
+    loads[3].wait()
+    west_side = jnp.logical_or(comp == 0, comp == COMP_AXIS - 1)
+    south_side = comp < 2
+    near_first = jnp.where(first_core, RIM + PTS, 0)
+    far_first = jnp.where(first_core, 0, RIM + PTS)
+    for axis, index in enumerate(
+        (
+            jnp.where(west_side, links[0:1], links[1:2]),
+            jnp.where(south_side, links[2:3], links[3:4]),
+        )
+    ):
+        no_left = jnp.logical_and(tile == 0, index < RIM)
+        no_right = jnp.logical_and(tile == tiles - 1, index >= RIM + PTS)
+        nothing = jnp.logical_or(jnp.logical_or(no_left, no_right), mask[...] == 0)
+        index = jnp.where(nothing, EXT, index)
+        lanes = pl.ds(axis * PTS, PTS)
+        table[0:PTS, lanes] = onehot(RIM, PTS, index)
+        table[PTS : PTS + RIM, lanes] = onehot(near_first, RIM, index)
+        table[PTS + RIM : EXT, lanes] = onehot(far_first, RIM, index)
+    counted = lax.broadcasted_iota(jnp.int32, (RIM, RIM), 0).astype(jnp.float32)
+    for axis in range(2):
+        picked = jnp.dot(
+            table[:, axis * PTS : (axis + 1) * PTS], picker, preferred_element_type=jnp.float32
+        )
+        for side in (NEAR, FAR):
+            lanes = slice(RIM * (2 * side + axis), RIM * (2 * side + axis + 1))
+            chosen = picked[:, side * RIM : (side + 1) * RIM]
+            send_table[:, lanes] = chosen.astype(jnp.bfloat16)
+        block = picked[PTS + RIM : EXT, RIM : 2 * RIM]
+        spots[:, axis * RIM : (axis + 1) * RIM] = float(RIM) + jnp.sum(
+            block * (counted - float(RIM)), axis=0, keepdims=True
+        )
+    spot_copy = pltpu.make_async_remote_copy(
+        src_ref=spots,
+        dst_ref=far_spots,
+        send_sem=spot_send,
+        recv_sem=spot_recv,
+        device_id=(far_tile, comp),
+        device_id_type=MESH,
+    )
+    pl.when(has_far)(lambda: spot_copy.start())
 
     loads[4].wait()
     diagonal = lax.broadcasted_iota(jnp.int32, (NK, NK), 0) == lax.broadcasted_iota(
@@ -191,51 +259,41 @@
         along[span] = speed_y
         keep[span] = 1.0 - speed_x - speed_y
 
-    loads[3].wait()
-    west_side = jnp.logical_or(comp == 0, comp == COMP_AXIS - 1)
-    south_side = comp < 2
-    for axis, index in enumerate(
-        (
-            jnp.where(west_side, links[0:1], links[1:2]),
-            jnp.where(south_side, links[2:3], links[3:4]),
-        )
-    ):
-        no_left = jnp.logical_and(tile == 0, index < RIM)
-        no_right = jnp.logical_and(tile == tiles - 1, index >= RIM + PTS)
-        nothing = jnp.logical_or(jnp.logical_or(no_left, no_right), mask[...] == 0)
-        index = jnp.where(nothing, EXT, index)
-        lanes = pl.ds(axis * PTS, PTS)
-        table[0:PTS, lanes] = onehot(RIM, PTS, index)
-        table[PTS : PTS + RIM, lanes] = onehot(0, RIM, index)
-        table[PTS + RIM : EXT, lanes] = onehot(RIM + PTS, RIM, index)
-    for axis in range(2):
-        picked = jnp.dot(
-            table[:, axis * PTS : (axis + 1) * PTS],
-            send_table[...],
-            preferred_element_type=jnp.float32,
-        )
-        first = OWN_N + axis * 2 * RIM
-        table[:, first : first + 2 * RIM] = picked.astype(jnp.bfloat16)
-
-    def own_part(group, split, values, sends, with_sends):
-        first, last = (GROUPS[group][0] * NK, GROUPS[group][1] * NK)
-        span = slice(first, last)
-        picked = gathered(split, table[0:PTS, 0:OWN_N])
-        pending[span] = (
-            wide(keep[span], PTS) * values
-            + wide(across[span], PTS) * picked[:, :PTS]
-            + wide(along[span], PTS) * picked[:, PTS:]
-        )
-        if with_sends:
-            picked = gathered(split, table[0:PTS, OWN_N:])
-            pending_send[span] = (
-                wide(keep[span], 2 * RIM) * sends
-                + wide(across[span], 2 * RIM) * picked[:, : 2 * RIM]
-                + wide(along[span], 2 * RIM) * picked[:, 2 * RIM :]
-            )
-
-    for group, (first, last) in enumerate(GROUPS):
-        own_part(group, splits[group], spec[first * NK : last * NK], first_sends[group], True)
+    def weighed(group, picked):
+        span = span_of(group)
+        lanes = picked.shape[1] // 2
+        return (
+            wide(across[span], lanes) * picked[:, :lanes]
+            + wide(along[span], lanes) * picked[:, lanes:]
+        )
+
+    def from_points(group, split, places):
+        return weighed(group, gathered(split, table[places, :]))
+
+    def from_sends(group, split, places, side):
+        lanes = slice(2 * RIM * side, 2 * RIM * (side + 1))
+        return weighed(group, gathered(split, send_table[places, lanes]))
+
+    OWN, NEAR_ROWS, FAR_ROWS, RIMS = (
+        slice(0, PTS),
+        slice(PTS, PTS + RIM),
+        slice(PTS + RIM, EXT),
+        slice(PTS, EXT),
+    )
+
+    def own_part(group, values, sends):
+        span = span_of(group)
+        split = halves(values)
+        pending[span] = wide(keep[span], PTS) * values + from_points(group, split, OWN)
+        if sends is not None:
+            for side in (NEAR, FAR):
+                pending_send[side, span] = keep[span] * sends[side] + from_sends(
+                    group, split, OWN, side
+                )
+
+    for group in range(len(GROUPS)):
+        sends = first_sends[group]
+        own_part(group, spec[span_of(group)], (sends[:, :RIM], sends[:, RIM:]))
 
     for number in (5, 6, 7, 8):
         loads[number].wait()
@@ -246,9 +304,11 @@
     angle = (lax.broadcasted_iota(jnp.int32, (8, PTS), 0) + comp * DIRS).astype(jnp.float32) * STEP
     aligned = jnp.cos(angle - wdir[...])
     driven = wind[...] * sigma
-    for d in range(DIRS):
-        grown = 0.4 * jnp.maximum(driven * aligned[d : d + 1] - 0.3, 0.0)
-        gain[d * NK : (d + 1) * NK] = wet * (1.0 + grown)
+
+    def wind_part():
+        for d in range(DIRS):
+            grown = 0.4 * jnp.maximum(driven * aligned[d : d + 1] - 0.3, 0.0)
+            gain[d * NK : (d + 1) * NK] = wet * (1.0 + grown)
 
     ghost_copies = [
         pltpu.make_async_remote_copy(
@@ -262,29 +322,54 @@
         for slot, at, target in ((0, DIRS - 1, comp_at[1]), (1, 0, comp_at[3]))
     ]
 
-    for step in range(NSUB):
+    for level in range(0, NSUB, 2):
+        more = level + 2 < NSUB
+        for group in range(len(GROUPS)):
+            span = span_of(group)
+            await_halo(level, NEAR, group)
+            split = halves(rim[level, NEAR, span])
+            sends = pending_send[FAR, span] + from_sends(group, split, NEAR_ROWS, FAR)
+            send_halo(level + 1, FAR, group, sends)
+            pending_send[NEAR, span] = pending_send[NEAR, span] + from_sends(
+                group, split, NEAR_ROWS, NEAR
+            )
+            pending[span] = pending[span] + from_points(group, split, NEAR_ROWS)
+        if level == 0:
+            wind_part()
+            pl.when(has_far)(lambda: spot_copy.wait_recv())
+            places = lax.broadcasted_iota(jnp.int32, (RIM, 2 * RIM), 0).astype(jnp.float32)
+            far_table[...] = jnp.where(places == far_spots[...], 1.0, 0.0).astype(jnp.bfloat16)
+        for group in range(len(GROUPS)):
+            span = span_of(group)
+            mended[span] = weighed(
+                group, gathered(halves(outgoing[level, FAR, span]), far_table[...])
+            )
+        for group in range(len(GROUPS)):
+            span = span_of(group)
+            await_halo(level, FAR, group)
+            split = halves(rim[level, FAR, span])
+            near = pending_send[NEAR, span] + from_sends(group, split, FAR_ROWS, NEAR)
+            send_halo(level + 1, NEAR, group, near)
+            far = None
+            if more:
+                far = outgoing[level + 1, FAR, span] + from_sends(group, split, FAR_ROWS, FAR)
+            values = pending[span] + from_points(group, split, FAR_ROWS)
+            own_part(group, values, (near, far) if more else None)
         for group, (low, high) in enumerate(GROUPS):
-            first, last = (low * NK, high * NK)
-            span = slice(first, last)
-            for copy in halo_copies(step, group):
-                copy.wait_recv()
-            split = halves(jnp.concatenate([rim[step, 0, span], rim[step, 1, span]], axis=1))
-            if step < NSUB - 1:
-                picked = gathered(split, table[PTS:EXT, OWN_N:])
-                sends = (
-                    pending_send[span]
-                    + wide(across[span], 2 * RIM) * picked[:, : 2 * RIM]
-                    + wide(along[span], 2 * RIM) * picked[:, 2 * RIM :]
-                )
-                send_halo(step + 1, group, sends)
-            picked = gathered(split, table[PTS:EXT, 0:OWN_N])
-            values = (
-                pending[span]
-                + wide(across[span], PTS) * picked[:, :PTS]
-                + wide(along[span], PTS) * picked[:, PTS:]
-            )
-            if step < NSUB - 1:
-                own_part(group, halves(values), values, sends, step < NSUB - 2)
+            span = span_of(group)
+            await_halo(level + 1, FAR, group)
+            far_rim = rim[level + 1, FAR, span] + mended[span]
+            await_halo(level + 1, NEAR, group)
+            split = halves(jnp.concatenate([rim[level + 1, NEAR, span], far_rim], axis=1))
+            if more:
+                sends = []
+                for side in (FAR, NEAR):
+                    values = pending_send[side, span] + from_sends(group, split, RIMS, side)
+                    send_halo(level + 2, side, group, values)
+                    sends.append(values)
+            values = pending[span] + from_points(group, split, RIMS)
+            if more:
+                own_part(group, values, (sends[1], sends[0]))
             else:
                 spec[span] = values
                 if low == 0:
@@ -351,8 +436,13 @@
         span = slice(d * NK, (d + 1) * NK)
         out_ref[span] = gain[span] * factor
 
-    for copy in started + ghost_copies + part_copies:
+    for copy in ghost_copies + part_copies:
         copy.wait_send()
+    pl.when(has_far)(lambda: spot_copy.wait_send())
+    for level in range(NSUB):
+        for side in (NEAR, FAR):
+            for group in range(len(GROUPS)):
+                only_if_far(side, lambda: halo_copy(level, side, group).wait_send())
 
 
 def shards(
@@ -377,7 +467,7 @@
     return pl.pallas_call(
         kernel,
         out_shape=jax.ShapeDtypeStruct((ROWS, PTS), f32),
-        in_specs=[pl.BlockSpec(memory_space=pl.ANY)] * 9,
+        in_specs=[pl.BlockSpec(memory_space=pltpu.HBM)] * 9,
         out_specs=pl.BlockSpec(memory_space=pltpu.VMEM),
         scratch_shapes=[
             vmem((ROWS, PTS), f32),
@@ -389,29 +479,35 @@
             vmem((1, PTS), jnp.int32),
             vmem((4, PTS), jnp.int32),
             vmem((1, 2 * RIM), jnp.int32),
-            vmem((EXT, OWN_N + SEND_N), jnp.bfloat16),
-            vmem((PTS, 2 * RIM), jnp.bfloat16),
+            vmem((EXT, OWN_N), jnp.bfloat16),
+            vmem((EXT, SEND_N), jnp.bfloat16),
+            vmem((RIM, 2 * RIM), jnp.bfloat16),
             vmem((ROWS, RIM), f32),
             vmem((ROWS, RIM), f32),
             vmem((ROWS, RIM), f32),
             vmem((NSUB, 2, ROWS, RIM), f32),
             vmem((NSUB, 2, ROWS, RIM), f32),
             vmem((ROWS, PTS), f32),
-            vmem((ROWS, 2 * RIM), f32),
+            vmem((2, ROWS, RIM), f32),
+            vmem((ROWS, RIM), f32),
             vmem((ROWS, PTS), f32),
             vmem((2, NK, PTS), f32),
             vmem((2, PTS), f32),
             vmem((3, 2, PTS), f32),
+            vmem((1, 2 * RIM), f32),
+            vmem((1, 2 * RIM), f32),
             dma((9,)),
-            dma((NSUB, groups, 2)),
-            dma((NSUB, groups, 2)),
+            dma((NSUB, 2, groups)),
+            dma((NSUB, 2, groups)),
             dma((2,)),
             dma((2,)),
             dma((3,)),
             dma((3,)),
+            dma,
+            dma,
         ],
         compiler_params=pltpu.CompilerParams(
-            collective_id=0, has_side_effects=True, vmem_limit_bytes=48 * 1024 * 1024
+            collective_id=0, has_side_effects=True, vmem_limit_bytes=60 * 1024 * 1024
         ),
         name="wave_step",
     )(

time: 37.5 us -> 27.4 us (0.73)
  the two profiles are of different devices: /device:TPU:8 before, /device:TPU:6 now
where the time goes in v2:
time: 27.4 us; the launch traced here: 27.2 us
  Pallas kernels  25.5 us (93%)
  local copies, waits for them, and re-layouts  1.77 us (6%)
    pallas_call x1, Pallas kernels, shards(): pl.pallas_call(kernel, out_shape=jax.ShapeDtypeStruct((ROWS, PTS), f32),...  25.5 us
    unnamed x1, local copies, waits for them, and re-layouts  1.77 us

profile of v2, /device:TPU:6, one launch (start us, length us, event | category | flops | bytes accessed | tf_op | source)
XLA Modules:
  0.0 27.2 jit_solution(6840398486172333542)
XLA Ops:
  0.0 25.5 %wave_step.1 = f32[192,512]{1,0:T(8,128)} custom-call(f32[192,512]{1,0:T(8,128)} %action_hbm.1, f32[1,32]{1,0:T(1,128)} %bitcast.13, f32[1,512]{1,0:T(1,128)} %bitcast.7, f32[1,512]{1,0:T(1,128)} %bitcast.8, f32[1,512]{1,0:T(1,128)} %bitcast.9, f32[1,512]{1,0:T(1,128)} %bitcast.10, s32[1,512]{1,0:T(1,128)} %bitcast.11, s32[4,512]{1,0:T(4,128)} %links_hbm.1, ...), custom_call_target="tpu_custom_call" | custom-call | tf_op jit(solution)/shard_map/wave_step/pallas_call | solution.py:467
  25.5 1.8 %copy.11 = f32[192,512]{1,0:T(8,128)} copy(f32[192,512]{1,0:T(8,128)} %wave_step.1) | data formatting | bytes 786432

commit v3 on v2

v3 whole, which is shorter than its diff:
```python
import functools
import math

import jax
import jax.numpy as jnp
import numpy as np
from jax import lax
from jax.experimental import pallas as pl
from jax.experimental.pallas import tpu as pltpu
from jax.sharding import PartitionSpec as P

NSUB = 4
NTH = 24
NK = 32
PTS = 512
RIM = 128
EXT = PTS + 2 * RIM
COMP_AXIS = 4
DIRS = NTH // COMP_AXIS
ROWS = DIRS * NK
COMPS = NTH * NK
OWN_N = 2 * PTS
NEAR, FAR = 0, 1
GROUPS = ((0, 6),)
MESH = pl.DeviceIdType.MESH
STEP = np.float32(2.0 * math.pi / NTH)
LOG_RATIO = np.float32(math.log(1.1))


def pick(index, values):
    chosen = jnp.float32(values[0])
    for place in range(1, len(values)):
        chosen = jnp.where(index == place, jnp.float32(values[place]), chosen)
    return chosen


def halves(values):
    high = values.astype(jnp.bfloat16)
    low = (values - high.astype(jnp.float32)).astype(jnp.bfloat16)
    return jnp.concatenate([high, low], axis=0)


def gathered(split, table):
    both = jnp.dot(split, table, preferred_element_type=jnp.float32)
    rows = both.shape[0] // 2
    return both[:rows] + both[rows:]


def wide(column, lanes):
    return jnp.concatenate([column] * (lanes // RIM), axis=1)


def onehot(first, count, index):
    places = lax.broadcasted_iota(jnp.int32, (count, index.shape[1]), 0) + first
    return jnp.where(places == index, 1.0, 0.0).astype(jnp.bfloat16)


def kernel(
    row_of_tiles,
    action_hbm,
    speed_hbm,
    turning_hbm,
    shift_hbm,
    wind_hbm,
    dir_hbm,
    mask_hbm,
    links_hbm,
    rows_hbm,
    out_ref,
    spec,
    speed,
    turning,
    shift,
    wind,
    wdir,
    mask,
    links,
    rows,
    table,
    send_table,
    back_table,
    across,
    along,
    keep,
    outgoing,
    rim,
    pending,
    pending_send,
    lists,
    mended,
    gain,
    ghost,
    part,
    parts,
    spots,
    back_spots,
    load_sem,
    halo_send,
    halo_recv,
    ghost_send,
    ghost_recv,
    part_send,
    part_recv,
    spot_send,
    spot_recv,
    two_on,
):
    tile = lax.axis_index("tiles")
    comp = lax.axis_index("comp")
    tiles = lax.axis_size("tiles")
    first_core = lax.rem(tile, 2) == 0
    near_tile = jnp.where(first_core, tile + 1, tile - 1)
    far_tile = jnp.where(first_core, tile - 1, tile + 1)
    has_far = jnp.logical_and(far_tile >= 0, far_tile < tiles)
    far_tile = jnp.clip(far_tile, 0, tiles - 1)
    comp_at = [lax.rem(comp + step, COMP_AXIS) for step in range(COMP_AXIS)]

    barrier = pltpu.get_barrier_semaphore()
    for place in (
        (near_tile, comp),
        (tile, comp_at[1]),
        (tile, comp_at[3]),
    ):
        pl.semaphore_signal(barrier, inc=1, device_id=place, device_id_type=MESH)

    @pl.when(has_far)
    def _():
        pl.semaphore_signal(barrier, inc=1, device_id=(far_tile, comp), device_id_type=MESH)

    loads = [
        pltpu.make_async_copy(source, target, load_sem.at[number])
        for number, (source, target) in enumerate(
            (
                (rows_hbm, rows),
                (mask_hbm, mask),
                (action_hbm, spec),
                (links_hbm, links),
                (speed_hbm, speed),
                (turning_hbm, turning),
                (shift_hbm, shift),
                (wind_hbm, wind),
                (dir_hbm, wdir),
            )
        )
    ]
    for load in loads:
        load.start()

    def span_of(group):
        return slice(GROUPS[group][0] * NK, GROUPS[group][1] * NK)

    def tile_at(side):
        if isinstance(side, int):
            return near_tile if side == NEAR else far_tile
        return jnp.where(side == NEAR, near_tile, far_tile)

    def halo_copy(level, side, group):
        first, last = (GROUPS[group][0] * NK, GROUPS[group][1] * NK)
        span = pl.ds(first, last - first)
        return pltpu.make_async_remote_copy(
            src_ref=outgoing.at[level, side, span],
            dst_ref=rim.at[level, side, span],
            send_sem=halo_send.at[level, side, group],
            recv_sem=halo_recv.at[level, side, group],
            device_id=(tile_at(side), comp),
            device_id_type=MESH,
        )

    def only_if_far(side, action):
        if side == NEAR:
            action()
        else:
            pl.when(has_far)(action)

    def send_halo(level, side, group, values):
        outgoing[level, side, span_of(group)] = values
        only_if_far(side, lambda: halo_copy(level, side, group).start())

    def await_halo(level, side, group):
        only_if_far(side, lambda: halo_copy(level, side, group).wait_recv())

    OWN, NEAR_ROWS, FAR_ROWS = (slice(0, PTS), slice(PTS, PTS + RIM), slice(PTS + RIM, EXT))
    RIMS = slice(PTS, EXT)
    SIDES = (FAR, NEAR)
    groups = range(len(GROUPS))

    loads[0].wait()
    low_rows, high_rows = (rows[:, 0:RIM], rows[:, RIM : 2 * RIM])
    near_rows = jnp.where(first_core, high_rows, low_rows)
    far_rows = jnp.where(first_core, low_rows, high_rows)
    picker = onehot(0, PTS, jnp.concatenate([near_rows, far_rows], axis=1))

    loads[1].wait()
    wet = mask[...].astype(jnp.float32)
    loads[3].wait()
    west_side = jnp.logical_or(comp == 0, comp == COMP_AXIS - 1)
    south_side = comp < 2
    near_first = jnp.where(first_core, RIM + PTS, 0)
    far_first = jnp.where(first_core, 0, RIM + PTS)
    for axis, index in enumerate(
        (
            jnp.where(west_side, links[0:1], links[1:2]),
            jnp.where(south_side, links[2:3], links[3:4]),
        )
    ):
        no_left = jnp.logical_and(tile == 0, index < RIM)
        no_right = jnp.logical_and(tile == tiles - 1, index >= RIM + PTS)
        nothing = jnp.logical_or(jnp.logical_or(no_left, no_right), mask[...] == 0)
        index = jnp.where(nothing, EXT, index)
        lanes = pl.ds(axis * PTS, PTS)
        table[0:PTS, lanes] = onehot(RIM, PTS, index)
        table[PTS : PTS + RIM, lanes] = onehot(near_first, RIM, index)
        table[PTS + RIM : EXT, lanes] = onehot(far_first, RIM, index)
    counted = lax.broadcasted_iota(jnp.int32, (RIM, RIM), 0).astype(jnp.float32)
    for axis in range(2):
        picked = jnp.dot(
            table[:, axis * PTS : (axis + 1) * PTS], picker, preferred_element_type=jnp.float32
        )
        for side in (NEAR, FAR):
            lanes = slice(RIM * axis, RIM * (axis + 1))
            chosen = picked[:, side * RIM : (side + 1) * RIM]
            send_table[side, :, lanes] = chosen.astype(jnp.bfloat16)
        for side, places in ((NEAR, NEAR_ROWS), (FAR, FAR_ROWS)):
            block = picked[places, side * RIM : (side + 1) * RIM]
            spots[side, :, axis * RIM : (axis + 1) * RIM] = float(RIM) + jnp.sum(
                block * (counted - float(RIM)), axis=0, keepdims=True
            )

    loads[4].wait()
    diagonal = lax.broadcasted_iota(jnp.int32, (NK, NK), 0) == lax.broadcasted_iota(
        jnp.int32, (NK, NK), 1
    )
    courant = jnp.sum(jnp.where(diagonal, speed[...], 0.0), axis=1, keepdims=True)
    courant = jnp.broadcast_to(courant, (NK, RIM))
    angles = np.arange(NTH).astype(np.float32) * STEP
    cosines = np.abs(np.cos(angles)).reshape(COMP_AXIS, DIRS)
    sines = np.abs(np.sin(angles)).reshape(COMP_AXIS, DIRS)
    for d in range(DIRS):
        span = slice(d * NK, (d + 1) * NK)
        speed_x = courant * pick(comp, cosines[:, d])
        speed_y = courant * pick(comp, sines[:, d])
        across[span] = speed_x
        along[span] = speed_y
        keep[span] = 1.0 - speed_x - speed_y

    def weighed(span, picked):
        lanes = picked.shape[1] // 2
        return (
            wide(across[span], lanes) * picked[:, :lanes]
            + wide(along[span], lanes) * picked[:, lanes:]
        )

    def from_points(span, split, places):
        return weighed(span, gathered(split, table[places, :]))

    def from_sends(span, split, places, side):
        return weighed(span, gathered(split, send_table[side, places]))

    def own_points(span, split, values):
        pending[span] = wide(keep[span], PTS) * values + from_points(span, split, OWN)

    def own_sends(level, span, split, side, values):
        lists[side, span] = values
        pending_send[level % 2, side, span] = keep[span] * values + from_sends(
            span, split, OWN, side
        )

    def mend(span, side):
        return weighed(span, gathered(halves(lists[side, span]), back_table[side]))

    loads[2].wait()
    spec[...] = spec[...] * wet
    splits = []
    for group in groups:
        split = halves(spec[span_of(group)])
        splits.append(split)
        first = gathered(split, picker)
        outgoing[0, NEAR, span_of(group)] = first[:, :RIM]
        outgoing[0, FAR, span_of(group)] = first[:, RIM:]
    for group in groups:
        for side in SIDES:
            own_sends(0, span_of(group), splits[group], side, outgoing[0, side, span_of(group)])

    @pl.when(jnp.logical_not(has_far))
    def _():
        for level in range(NSUB):
            rim[level, FAR] = jnp.zeros((ROWS, RIM), jnp.float32)
        back_spots[FAR] = jnp.full((1, 2 * RIM), float(RIM), jnp.float32)

    spot_copies = [
        pltpu.make_async_remote_copy(
            src_ref=spots.at[side],
            dst_ref=back_spots.at[side],
            send_sem=spot_send.at[side],
            recv_sem=spot_recv.at[side],
            device_id=(near_tile if side == NEAR else far_tile, comp),
            device_id_type=MESH,
        )
        for side in (NEAR, FAR)
    ]

    pl.semaphore_wait(barrier, jnp.where(has_far, 4, 3))
    for side in SIDES:
        only_if_far(side, lambda: spot_copies[side].start())
        for group in groups:
            only_if_far(side, lambda: halo_copy(0, side, group).start())

    pl.semaphore_signal(two_on, inc=1, device_id=(tile, comp_at[3]), device_id_type=MESH)

    ghost_copies = [
        pltpu.make_async_remote_copy(
            src_ref=spec.at[pl.ds(at * NK, NK)],
            dst_ref=ghost.at[slot],
            send_sem=ghost_send.at[slot],
            recv_sem=ghost_recv.at[slot],
            device_id=(tile, target),
            device_id_type=MESH,
        )
        for slot, at, target in ((0, DIRS - 1, comp_at[1]), (1, 0, comp_at[3]))
    ]

    spans = [span_of(group) for group in groups]

    def whole_rim(level, side, group):
        values = rim[level, side, spans[group]]
        if (level, side) in ((1, FAR), (2, FAR), (2, NEAR), (3, FAR)):
            values = values + mended[side, spans[group]]
        return values

    def arrived(level, side, group):
        await_halo(level, side, group)
        return halves(whole_rim(level, side, group))

    def for_far(level, span, near):
        return pending_send[level % 2, FAR, span] + from_sends(span, near, NEAR_ROWS, FAR)

    def whole_list(level, span, side, both):
        return pending_send[level % 2, side, span] + from_sends(span, both, RIMS, side)

    def joined(near, far):
        return jnp.concatenate([near, far], axis=1)

    def next_points(span, both):
        return pending[span] + from_points(span, both, RIMS)

    near_0 = []
    for group in groups:
        near_0.append(arrived(0, NEAR, group))
        send_halo(1, FAR, group, for_far(0, spans[group], near_0[group]))
    for group, span in enumerate(spans):
        own_points(span, splits[group], spec[span])
    for number in (5, 6, 7, 8):
        loads[number].wait()
    sigma = jnp.exp(
        (lax.broadcasted_iota(jnp.int32, (NK, RIM), 0) - NK // 2).astype(jnp.float32) * LOG_RATIO
    )
    sigma = wide(sigma, PTS)
    angle = (lax.broadcasted_iota(jnp.int32, (8, PTS), 0) + comp * DIRS).astype(jnp.float32) * STEP
    aligned = jnp.cos(angle - wdir[...])
    driven = wind[...] * sigma
    for d in range(DIRS):
        grown = 0.4 * jnp.maximum(driven * aligned[d : d + 1] - 0.3, 0.0)
        gain[d * NK : (d + 1) * NK] = wet * (1.0 + grown)
    places = lax.broadcasted_iota(jnp.int32, (RIM, 2 * RIM), 0).astype(jnp.float32)
    for side in SIDES:
        only_if_far(side, lambda: spot_copies[side].wait_recv())
        back_table[side] = jnp.where(places == back_spots[side], 1.0, 0.0).astype(jnp.bfloat16)
    for span in spans:
        mended[FAR, span] = mend(span, FAR)
    split_1 = []
    points_1 = []
    near_list_1 = []
    for group, span in enumerate(spans):
        both = joined(near_0[group], arrived(0, FAR, group))
        near_list_1.append(whole_list(0, span, NEAR, both))
        far_list_1 = whole_list(0, span, FAR, both)
        points_1.append(next_points(span, both))
        send_halo(1, NEAR, group, near_list_1[group])
        split_1.append(halves(points_1[group]))
        own_sends(1, span, split_1[group], FAR, far_list_1)

    can_wait = lax.rem(tile, row_of_tiles) == row_of_tiles - 1

    def near_list_work():
        for group, span in enumerate(spans):
            own_sends(1, span, split_1[group], NEAR, near_list_1[group])

    pl.when(jnp.logical_not(can_wait))(near_list_work)
    first_side = jnp.where(first_core, FAR, NEAR)

    def await_side(side):
        for group in groups:
            pl.when(jnp.logical_or(side == NEAR, has_far))(
                lambda: halo_copy(1, side, group).wait_recv()
            )

    def send_past(side):
        other = 1 - side
        for group, span in enumerate(spans):
            share = jnp.where(side == FAR, mended[FAR, span], 0.0)
            split = halves(rim[1, side, span] + share)
            rows_of_side = pl.ds(pl.multiple_of(PTS + RIM * side, RIM), RIM)
            outgoing[2, other, span] = pending_send[1, other, span] + weighed(
                span, gathered(split, send_table[other, rows_of_side])
            )
            pl.when(jnp.logical_or(other == NEAR, has_far))(
                lambda: halo_copy(2, other, group).start()
            )

    await_side(first_side)
    send_past(first_side)
    await_side(1 - first_side)
    pl.when(jnp.logical_not(can_wait))(lambda: send_past(1 - first_side))
    points_2 = []
    split_2 = []
    near_1 = []
    both_1 = []
    for group, span in enumerate(spans):
        near_1.append(halves(whole_rim(1, NEAR, group)))
        both_1.append(joined(near_1[group], halves(whole_rim(1, FAR, group))))
        values = wide(keep[span], PTS) * points_1[group] + from_points(
            span, joined(split_1[group], both_1[group]), slice(0, EXT)
        )
        whole = whole_list(1, span, FAR, both_1[group])
        points_2.append(values)
        split_2.append(halves(values))
        far_share = mend(span, FAR)
        mended[FAR, span] = far_share
        own_sends(2, span, split_2[group], FAR, whole)
        lists[NEAR, span] = near_list_1[group]
        mended[NEAR, span] = mend(span, NEAR)

    near_2 = []
    for group, span in enumerate(spans):
        near_2.append(arrived(2, NEAR, group))
        send_halo(3, FAR, group, for_far(2, span, near_2[group]))

    @pl.when(can_wait)
    def _():
        near_list_work()
        for group, span in enumerate(spans):
            far = both_1[group][:, RIM:]
            sends = pending_send[1, NEAR, span] + from_sends(span, far, FAR_ROWS, NEAR)
            send_halo(2, NEAR, group, sends)

    for group, span in enumerate(spans):
        near_list_2 = whole_list(1, span, NEAR, both_1[group])
        own_sends(2, span, split_2[group], NEAR, near_list_2)
        own_points(span, split_2[group], points_2[group])
    for group, span in enumerate(spans):
        both = joined(near_2[group], arrived(2, FAR, group))
        sends = whole_list(2, span, NEAR, both)
        values = next_points(span, both)
        send_halo(3, NEAR, group, sends)
        own_points(span, halves(values), values)
        mended[FAR, span] = mend(span, FAR)

    near_3 = [arrived(3, NEAR, group) for group in groups]
    far_3 = [arrived(3, FAR, group) for group in groups]
    for group, (low, high) in enumerate(GROUPS):
        span = spans[group]
        spec[span] = next_points(span, joined(near_3[group], far_3[group]))
        if low == 0:
            ghost_copies[1].start()
        if high == DIRS:
            ghost_copies[0].start()

    turn = turning[...]
    moved = shift[...]
    freq = lax.broadcasted_iota(jnp.int32, (NK, PTS), 0)

    def shifted(values):
        lower = jnp.where(freq == 0, 0.0, pltpu.roll(values, 1, 0))
        upper = jnp.where(freq == NK - 1, 0.0, pltpu.roll(values, NK - 1, 0))
        return values - jnp.abs(moved) * (values - jnp.where(moved > 0, lower, upper))

    total = spec[0:NK]
    for d in range(1, DIRS):
        total = total + spec[d * NK : (d + 1) * NK]
    total = shifted(total) * sigma
    energy = jnp.sum(total, axis=0, keepdims=True)
    moment = jnp.sum(total * sigma, axis=0, keepdims=True)
    part[0:1] = energy
    part[1:2] = moment
    part_copies = [
        pltpu.make_async_remote_copy(
            src_ref=part,
            dst_ref=parts.at[hop - 1],
            send_sem=part_send.at[hop - 1],
            recv_sem=part_recv.at[hop - 1],
            device_id=(tile, comp_at[hop]),
            device_id_type=MESH,
        )
        for hop in (2, 1, 3)
    ]
    pl.semaphore_wait(two_on, 1)
    for copy in part_copies:
        copy.start()

    def refracted(d):
        values = spec[d * NK : (d + 1) * NK]
        before = ghost[0] if d == 0 else spec[(d - 1) * NK : d * NK]
        beyond = ghost[1] if d == DIRS - 1 else spec[(d + 1) * NK : (d + 2) * NK]
        return values - jnp.abs(turn) * (values - jnp.where(turn > 0, before, beyond))

    def grow(d):
        span = slice(d * NK, (d + 1) * NK)
        gain[span] = gain[span] * shifted(refracted(d))

    for d in range(1, DIRS - 1):
        grow(d)
    for copy in ghost_copies + part_copies:
        copy.wait_send()
    for side in SIDES:
        only_if_far(side, lambda: spot_copies[side].wait_send())
    for level in range(NSUB):
        for side in (NEAR, FAR):
            for group in range(len(GROUPS)):
                only_if_far(side, lambda: halo_copy(level, side, group).wait_send())
    ghost_copies[0].wait_recv()
    grow(0)
    ghost_copies[1].wait_recv()
    grow(DIRS - 1)
    for copy in part_copies:
        copy.wait_recv()
    whole = (part[...] + parts[0] + parts[1] + parts[2]) * jnp.float32(1.0 / COMPS)
    energy = whole[0:1]
    mean_freq = whole[1:2] / jnp.maximum(energy, 0.05)
    strength = mean_freq * mean_freq * mean_freq * energy * energy
    damping = 0.005 * (sigma * sigma) * strength
    factor = 1.0 / (1.0 + damping)
    for d in range(DIRS):
        span = slice(d * NK, (d + 1) * NK)
        out_ref[span] = gain[span] * factor


def shards(
    row_of_tiles,
    action,
    speed_courant,
    turning,
    freq_shift,
    wind_speed,
    wind_dir,
    sea_mask,
    neighbours,
    halo_rows,
):
    vmem = pltpu.VMEM
    f32 = jnp.float32
    dma = pltpu.SemaphoreType.DMA
    groups = len(GROUPS)

    def row(values):
        return values.reshape(1, values.shape[0])

    return pl.pallas_call(
        functools.partial(kernel, row_of_tiles),
        out_shape=pltpu.VMEM((ROWS, PTS), f32),
        in_specs=[pl.BlockSpec(memory_space=pltpu.HBM)] * 9,
        out_specs=pl.BlockSpec(memory_space=pltpu.VMEM),
        scratch_shapes=[
            vmem((ROWS, PTS), f32),
            vmem((1, NK), f32),
            vmem((1, PTS), f32),
            vmem((1, PTS), f32),
            vmem((1, PTS), f32),
            vmem((1, PTS), f32),
            vmem((1, PTS), jnp.int32),
            vmem((4, PTS), jnp.int32),
            vmem((1, 2 * RIM), jnp.int32),
            vmem((EXT, OWN_N), jnp.bfloat16),
            vmem((2, EXT, 2 * RIM), jnp.bfloat16),
            vmem((2, RIM, 2 * RIM), jnp.bfloat16),
            vmem((ROWS, RIM), f32),
            vmem((ROWS, RIM), f32),
            vmem((ROWS, RIM), f32),
            vmem((NSUB, 2, ROWS, RIM), f32),
            vmem((NSUB, 2, ROWS, RIM), f32),
            vmem((ROWS, PTS), f32),
            vmem((2, 2, ROWS, RIM), f32),
            vmem((2, ROWS, RIM), f32),
            vmem((2, ROWS, RIM), f32),
            vmem((ROWS, PTS), f32),
            vmem((2, NK, PTS), f32),
            vmem((2, PTS), f32),
            vmem((3, 2, PTS), f32),
            vmem((2, 1, 2 * RIM), f32),
            vmem((2, 1, 2 * RIM), f32),
            dma((9,)),
            dma((NSUB, 2, groups)),
            dma((NSUB, 2, groups)),
            dma((2,)),
            dma((2,)),
            dma((3,)),
            dma((3,)),
            dma((2,)),
            dma((2,)),
            pltpu.SemaphoreType.REGULAR,
        ],
        compiler_params=pltpu.CompilerParams(
            collective_id=0, has_side_effects=True, vmem_limit_bytes=48 * 1024 * 1024
        ),
        name="wave_step",
    )(
        *(
            pltpu.with_memory_space_constraint(values, pltpu.HBM)
            for values in (
                action,
                row(speed_courant),
                row(turning),
                row(freq_shift),
                row(wind_speed),
                row(wind_dir),
                row(sea_mask),
                neighbours,
                row(halo_rows),
            )
        )
    )


def solution(mesh):
    placed = (
        P("comp", "tiles"),
        P(),
        P("tiles"),
        P("tiles"),
        P("tiles"),
        P("tiles"),
        P("tiles"),
        P(None, "tiles"),
        P("tiles"),
    )
    return jax.shard_map(
        functools.partial(shards, mesh.shape["tiles"] // COMP_AXIS), mesh=mesh, in_specs=placed, out_specs=P("comp", "tiles"), check_vma=False
    )
```

time: 27.4 us -> 23.8 us (0.87)
  Pallas kernels: 25.5 us -> 22.9 us
  local copies, waits for them, and re-layouts: 1.77 us -> 0.75 us
    pallas_call x1, Pallas kernels: 25.5 us -> 22.9 us  [shards(): pl.pallas_call(functools.partial(kernel, row_of_tiles), out_shape=pltpu.V...]
    unnamed x1, local copies, waits for them, and re-layouts: 1.77 us -> 0.75 us
where the time goes in v3:
time: 23.8 us; the launch traced here: 23.7 us
  Pallas kernels  22.9 us (96%)
  local copies, waits for them, and re-layouts  0.75 us (3%)
    pallas_call x1, Pallas kernels, shards(): pl.pallas_call(functools.partial(kernel, row_of_tiles), out_shape=pltpu.V...  22.9 us
    unnamed x1, local copies, waits for them, and re-layouts  0.75 us

profile of v3, /device:TPU:6, one launch (start us, length us, event | category | flops | bytes accessed | tf_op | source)
XLA Modules:
  0.0 23.7 jit_solution(12253006461105290634)
XLA Ops:
  0.0 22.9 %wave_step.1 = f32[192,512]{1,0:T(8,128)S(1)} custom-call(f32[192,512]{1,0:T(8,128)} %action_hbm.1, f32[1,32]{1,0:T(1,128)} %bitcast.13, f32[1,512]{1,0:T(1,128)} %bitcast.7, f32[1,512]{1,0:T(1,128)} %bitcast.8, f32[1,512]{1,0:T(1,128)} %bitcast.9, f32[1,512]{1,0:T(1,128)} %bitcast.10, s32[1,512]{1,0:T(1,128)} %bitcast.11, s32[4,512]{1,0:T(4,128)} %links_hbm.1, ...), custom_call_target="tpu_custom_call" | custom-call | tf_op jit(solution)/shard_map/wave_step/pallas_call | solution.py:557
  23.0 0.7 %copy.11 = f32[192,512]{1,0:T(8,128)} copy(f32[192,512]{1,0:T(8,128)S(1)} %wave_step.1) | data formatting | bytes 786432

commit v4 on v3

v4 whole, which is shorter than its diff:
```python
import functools
import math

import jax
import jax.numpy as jnp
import numpy as np
from jax import lax
from jax.experimental import pallas as pl
from jax.experimental.pallas import tpu as pltpu
from jax.sharding import PartitionSpec as P

NSUB = 4
NTH = 24
NK = 32
PTS = 512
RIM = 128
EXT = PTS + 2 * RIM
COMP_AXIS = 4
DIRS = NTH // COMP_AXIS
ROWS = DIRS * NK
COMPS = NTH * NK
OWN_N = 2 * PTS
NEAR, FAR = 0, 1
SPOT_ROWS = 8
MESH = pl.DeviceIdType.MESH
STEP = np.float32(2.0 * math.pi / NTH)
LOG_RATIO = np.float32(math.log(1.1))


def pick(index, values):
    chosen = jnp.float32(values[0])
    for place in range(1, len(values)):
        chosen = jnp.where(index == place, jnp.float32(values[place]), chosen)
    return chosen


def halves(values):
    high = values.astype(jnp.bfloat16)
    low = (values - high.astype(jnp.float32)).astype(jnp.bfloat16)
    return jnp.concatenate([high, low], axis=0)


def gathered(split, table):
    both = jnp.dot(split, table, preferred_element_type=jnp.float32)
    rows = both.shape[0] // 2
    return both[:rows] + both[rows:]


def wide(column, lanes):
    return jnp.concatenate([column] * (lanes // RIM), axis=1)


def onehot(first, count, index):
    places = lax.broadcasted_iota(jnp.int32, (count, index.shape[1]), 0) + first
    return jnp.where(places == index, 1.0, 0.0).astype(jnp.bfloat16)


def kernel(
    row_of_tiles,
    action_hbm,
    speed_hbm,
    turning_hbm,
    shift_hbm,
    wind_hbm,
    dir_hbm,
    mask_hbm,
    links_hbm,
    rows_hbm,
    out_ref,
    spec,
    speed,
    misc,
    mask,
    links,
    rows,
    table,
    send_table,
    back_table,
    across,
    along,
    keep,
    first_out,
    first_rim,
    outgoing,
    rim,
    pending,
    pending_send,
    lists,
    mended,
    gain,
    ghost,
    part,
    parts,
    local_sem,
    halo_recv,
    ghost_recv,
    part_recv,
    two_on,
):
    tile = lax.axis_index("tiles")
    comp = lax.axis_index("comp")
    tiles = lax.axis_size("tiles")
    first_core = lax.rem(tile, 2) == 0
    near_tile = jnp.where(first_core, tile + 1, tile - 1)
    far_tile = jnp.where(first_core, tile - 1, tile + 1)
    has_far = jnp.logical_and(far_tile >= 0, far_tile < tiles)
    far_tile = jnp.clip(far_tile, 0, tiles - 1)
    comp_at = [lax.rem(comp + step, COMP_AXIS) for step in range(COMP_AXIS)]

    barrier = pltpu.get_barrier_semaphore()
    for place in (
        (near_tile, comp),
        (tile, comp_at[1]),
        (tile, comp_at[3]),
    ):
        pl.semaphore_signal(barrier, inc=1, device_id=place, device_id_type=MESH)

    @pl.when(has_far)
    def _():
        pl.semaphore_signal(barrier, inc=1, device_id=(far_tile, comp), device_id_type=MESH)

    loads = [
        pltpu.make_async_copy(source, target, local_sem.at[number])
        for number, source, target in (
            (0, rows_hbm, rows),
            (1, mask_hbm, mask),
            (2, action_hbm, spec),
            (3, links_hbm, links),
            (4, speed_hbm, speed),
            (5, turning_hbm, misc.at[pl.ds(0, 1)]),
            (5, shift_hbm, misc.at[pl.ds(1, 1)]),
            (5, wind_hbm, misc.at[pl.ds(2, 1)]),
            (5, dir_hbm, misc.at[pl.ds(3, 1)]),
        )
    ]
    for load in loads:
        load.start()

    def await_bytes(ref, semaphore):
        pltpu.make_async_copy(ref, ref, semaphore).wait()

    near_sent, far_sent, ghost_sent, first_near_sent, first_far_sent, part_sent = (
        local_sem.at[number] for number in range(6)
    )

    def tile_at(side):
        if isinstance(side, int):
            return near_tile if side == NEAR else far_tile
        return jnp.where(side == NEAR, near_tile, far_tile)

    def halo_copy(level, side):
        if level == 0:
            source, target = (first_out.at[side], first_rim.at[side])
            sent = first_near_sent if side == NEAR else first_far_sent
        else:
            source, target = (outgoing.at[level - 1, side], rim.at[level - 1, side])
            sent = local_sem.at[side]
        return pltpu.make_async_remote_copy(
            src_ref=source,
            dst_ref=target,
            send_sem=sent,
            recv_sem=halo_recv.at[level, side],
            device_id=(tile_at(side), comp),
            device_id_type=MESH,
        )

    def only_if_far(side, action):
        if side == NEAR:
            action()
        else:
            pl.when(has_far)(action)

    def send_halo(level, side, values):
        outgoing[level - 1, side] = values
        only_if_far(side, lambda: halo_copy(level, side).start())

    def await_halo(level, side):
        only_if_far(side, lambda: halo_copy(level, side).wait_recv())

    OWN, NEAR_ROWS, FAR_ROWS = (slice(0, PTS), slice(PTS, PTS + RIM), slice(PTS + RIM, EXT))
    RIMS = slice(PTS, EXT)
    SIDES = (FAR, NEAR)

    loads[0].wait()
    low_rows, high_rows = (rows[:, 0:RIM], rows[:, RIM : 2 * RIM])
    near_rows = jnp.where(first_core, high_rows, low_rows)
    far_rows = jnp.where(first_core, low_rows, high_rows)
    picker = onehot(0, PTS, jnp.concatenate([near_rows, far_rows], axis=1))

    loads[1].wait()
    wet = mask[...].astype(jnp.float32)
    loads[3].wait()
    west_side = jnp.logical_or(comp == 0, comp == COMP_AXIS - 1)
    south_side = comp < 2
    near_first = jnp.where(first_core, RIM + PTS, 0)
    far_first = jnp.where(first_core, 0, RIM + PTS)
    for axis, index in enumerate(
        (
            jnp.where(west_side, links[0:1], links[1:2]),
            jnp.where(south_side, links[2:3], links[3:4]),
        )
    ):
        no_left = jnp.logical_and(tile == 0, index < RIM)
        no_right = jnp.logical_and(tile == tiles - 1, index >= RIM + PTS)
        nothing = jnp.logical_or(jnp.logical_or(no_left, no_right), mask[...] == 0)
        index = jnp.where(nothing, EXT, index)
        lanes = pl.ds(axis * PTS, PTS)
        table[0:PTS, lanes] = onehot(RIM, PTS, index)
        table[PTS : PTS + RIM, lanes] = onehot(near_first, RIM, index)
        table[PTS + RIM : EXT, lanes] = onehot(far_first, RIM, index)
    counted = lax.broadcasted_iota(jnp.int32, (RIM, RIM), 0).astype(jnp.float32)
    for axis in range(2):
        picked = jnp.dot(
            table[:, axis * PTS : (axis + 1) * PTS], picker, preferred_element_type=jnp.float32
        )
        for side in (NEAR, FAR):
            lanes = slice(RIM * axis, RIM * (axis + 1))
            chosen = picked[:, side * RIM : (side + 1) * RIM]
            send_table[side, :, lanes] = chosen.astype(jnp.bfloat16)
        for side, places in ((NEAR, NEAR_ROWS), (FAR, FAR_ROWS)):
            block = picked[places, side * RIM : (side + 1) * RIM]
            first_out[side, ROWS + axis : ROWS + axis + 1] = float(RIM) + jnp.sum(
                block * (counted - float(RIM)), axis=0, keepdims=True
            )

    loads[4].wait()
    diagonal = lax.broadcasted_iota(jnp.int32, (NK, NK), 0) == lax.broadcasted_iota(
        jnp.int32, (NK, NK), 1
    )
    courant = jnp.sum(jnp.where(diagonal, speed[...], 0.0), axis=1, keepdims=True)
    courant = jnp.broadcast_to(courant, (NK, RIM))
    angles = np.arange(NTH).astype(np.float32) * STEP
    cosines = np.abs(np.cos(angles)).reshape(COMP_AXIS, DIRS)
    sines = np.abs(np.sin(angles)).reshape(COMP_AXIS, DIRS)
    for d in range(DIRS):
        span = slice(d * NK, (d + 1) * NK)
        speed_x = courant * pick(comp, cosines[:, d])
        speed_y = courant * pick(comp, sines[:, d])
        across[span] = speed_x
        along[span] = speed_y
        keep[span] = 1.0 - speed_x - speed_y

    def weighed(picked):
        lanes = picked.shape[1] // 2
        return (
            wide(across[...], lanes) * picked[:, :lanes]
            + wide(along[...], lanes) * picked[:, lanes:]
        )

    def from_points(split, places):
        return weighed(gathered(split, table[places, :]))

    def from_sends(split, places, side):
        return weighed(gathered(split, send_table[side, places]))

    def own_points(split, values):
        pending[...] = wide(keep[...], PTS) * values + from_points(split, OWN)

    def own_sends(level, split, side, values):
        lists[side] = values
        pending_send[level % 2, side] = keep[...] * values + from_sends(split, OWN, side)

    def mend(side):
        return weighed(gathered(halves(lists[side]), back_table[side]))

    loads[2].wait()
    spec[...] = spec[...] * wet
    split_0 = halves(spec[...])
    first = gathered(split_0, picker)
    for side in SIDES:
        first_out[side, 0:ROWS] = first[:, side * RIM : (side + 1) * RIM]
        first_out[side, ROWS + 2 :] = jnp.zeros((SPOT_ROWS - 2, RIM), jnp.float32)
        own_sends(0, split_0, side, first[:, side * RIM : (side + 1) * RIM])

    @pl.when(jnp.logical_not(has_far))
    def _():
        for level in range(1, NSUB):
            rim[level - 1, FAR] = jnp.zeros((ROWS, RIM), jnp.float32)
        first_rim[FAR, 0:ROWS] = jnp.zeros((ROWS, RIM), jnp.float32)
        first_rim[FAR, ROWS:] = jnp.full((SPOT_ROWS, RIM), float(RIM), jnp.float32)

    pl.semaphore_wait(barrier, jnp.where(has_far, 4, 3))
    for side in SIDES:
        only_if_far(side, lambda: halo_copy(0, side).start())

    pl.semaphore_signal(two_on, inc=1, device_id=(tile, comp_at[3]), device_id_type=MESH)

    ghost_copies = [
        pltpu.make_async_remote_copy(
            src_ref=spec.at[pl.ds(at * NK, NK)],
            dst_ref=ghost.at[slot],
            send_sem=ghost_sent,
            recv_sem=ghost_recv,
            device_id=(tile, target),
            device_id_type=MESH,
        )
        for slot, at, target in ((0, DIRS - 1, comp_at[1]), (1, 0, comp_at[3]))
    ]

    def whole_rim(level, side):
        if level == 0:
            return first_rim[side, 0:ROWS]
        values = rim[level - 1, side]
        if (level, side) in ((1, FAR), (2, FAR), (2, NEAR), (3, FAR)):
            values = values + mended[side]
        return values

    def arrived(level, side):
        await_halo(level, side)
        return halves(whole_rim(level, side))

    def for_far(level, near):
        return pending_send[level % 2, FAR] + from_sends(near, NEAR_ROWS, FAR)

    def whole_list(level, side, both):
        return pending_send[level % 2, side] + from_sends(both, RIMS, side)

    def joined(near, far):
        return jnp.concatenate([near, far], axis=1)

    def next_points(both):
        return pending[...] + from_points(both, RIMS)

    near_0 = arrived(0, NEAR)
    send_halo(1, FAR, for_far(0, near_0))
    own_points(split_0, spec[...])
    await_bytes(misc, local_sem.at[5])
    sigma = jnp.exp(
        (lax.broadcasted_iota(jnp.int32, (NK, RIM), 0) - NK // 2).astype(jnp.float32) * LOG_RATIO
    )
    sigma = wide(sigma, PTS)
    angle = (lax.broadcasted_iota(jnp.int32, (8, PTS), 0) + comp * DIRS).astype(jnp.float32) * STEP
    aligned = jnp.cos(angle - misc[3:4])
    driven = misc[2:3] * sigma
    for d in range(DIRS):
        grown = 0.4 * jnp.maximum(driven * aligned[d : d + 1] - 0.3, 0.0)
        gain[d * NK : (d + 1) * NK] = wet * (1.0 + grown)
    far_0 = arrived(0, FAR)
    both_0 = joined(near_0, far_0)
    near_list_1 = whole_list(0, NEAR, both_0)
    far_list_1 = whole_list(0, FAR, both_0)
    points_1 = next_points(both_0)
    send_halo(1, NEAR, near_list_1)
    split_1 = halves(points_1)
    own_first = lists[FAR]
    own_sends(1, split_1, FAR, far_list_1)
    places = lax.broadcasted_iota(jnp.int32, (RIM, RIM), 0).astype(jnp.float32)
    for side in SIDES:
        for axis in range(2):
            spots = first_rim[side, ROWS + axis : ROWS + axis + 1]
            back_table[side, :, axis * RIM : (axis + 1) * RIM] = jnp.where(
                places == spots, 1.0, 0.0
            ).astype(jnp.bfloat16)
    mended[FAR] = weighed(gathered(halves(own_first), back_table[FAR]))

    can_wait = lax.rem(tile, row_of_tiles) == row_of_tiles - 1

    def near_list_work():
        own_sends(1, split_1, NEAR, near_list_1)

    pl.when(jnp.logical_not(can_wait))(near_list_work)
    first_side = jnp.where(first_core, FAR, NEAR)

    def await_side(side):
        pl.when(jnp.logical_or(side == NEAR, has_far))(lambda: halo_copy(1, side).wait_recv())

    def send_past(side):
        other = 1 - side
        share = jnp.where(side == FAR, mended[FAR], 0.0)
        split = halves(rim[0, side] + share)
        rows_of_side = pl.ds(pl.multiple_of(PTS + RIM * side, RIM), RIM)
        outgoing[1, other] = pending_send[1, other] + weighed(
            gathered(split, send_table[other, rows_of_side])
        )
        pl.when(jnp.logical_or(other == NEAR, has_far))(lambda: halo_copy(2, other).start())

    await_side(first_side)
    send_past(first_side)
    await_side(1 - first_side)
    pl.when(jnp.logical_not(can_wait))(lambda: send_past(1 - first_side))
    near_1 = halves(whole_rim(1, NEAR))
    far_1 = halves(whole_rim(1, FAR))
    both_1 = joined(near_1, far_1)
    points_2 = wide(keep[...], PTS) * points_1 + from_points(joined(split_1, both_1), slice(0, EXT))
    far_list_2 = whole_list(1, FAR, both_1)
    split_2 = halves(points_2)
    far_share = mend(FAR)
    mended[FAR] = far_share
    own_sends(2, split_2, FAR, far_list_2)
    lists[NEAR] = near_list_1
    mended[NEAR] = mend(NEAR)

    near_2 = arrived(2, NEAR)
    send_halo(3, FAR, for_far(2, near_2))

    @pl.when(can_wait)
    def _():
        near_list_work()
        send_halo(2, NEAR, pending_send[1, NEAR] + from_sends(far_1, FAR_ROWS, NEAR))

    own_sends(2, split_2, NEAR, whole_list(1, NEAR, both_1))
    own_points(split_2, points_2)
    both_2 = joined(near_2, arrived(2, FAR))
    near_list_3 = whole_list(2, NEAR, both_2)
    points_3 = next_points(both_2)
    send_halo(3, NEAR, near_list_3)
    own_points(halves(points_3), points_3)
    mended[FAR] = mend(FAR)

    near_3 = arrived(3, NEAR)
    spec[...] = next_points(joined(near_3, arrived(3, FAR)))
    for copy in ghost_copies:
        copy.start()

    turn = misc[0:1]
    moved = misc[1:2]
    freq = lax.broadcasted_iota(jnp.int32, (NK, PTS), 0)

    def shifted(values):
        lower = jnp.where(freq == 0, 0.0, pltpu.roll(values, 1, 0))
        upper = jnp.where(freq == NK - 1, 0.0, pltpu.roll(values, NK - 1, 0))
        return values - jnp.abs(moved) * (values - jnp.where(moved > 0, lower, upper))

    total = spec[0:NK]
    for d in range(1, DIRS):
        total = total + spec[d * NK : (d + 1) * NK]
    total = shifted(total) * sigma
    energy = jnp.sum(total, axis=0, keepdims=True)
    moment = jnp.sum(total * sigma, axis=0, keepdims=True)
    part[0:1] = energy
    part[1:2] = moment
    part_copies = [
        pltpu.make_async_remote_copy(
            src_ref=part,
            dst_ref=parts.at[hop - 1],
            send_sem=part_sent,
            recv_sem=part_recv,
            device_id=(tile, comp_at[hop]),
            device_id_type=MESH,
        )
        for hop in (2, 1, 3)
    ]
    pl.semaphore_wait(two_on, 1)
    for copy in part_copies:
        copy.start()

    def refracted(d):
        values = spec[d * NK : (d + 1) * NK]
        before = ghost[0] if d == 0 else spec[(d - 1) * NK : d * NK]
        beyond = ghost[1] if d == DIRS - 1 else spec[(d + 1) * NK : (d + 2) * NK]
        return values - jnp.abs(turn) * (values - jnp.where(turn > 0, before, beyond))

    def grow(d):
        span = slice(d * NK, (d + 1) * NK)
        gain[span] = gain[span] * shifted(refracted(d))

    for d in range(1, DIRS - 1):
        grow(d)
    await_bytes(ghost, ghost_sent)
    await_bytes(parts, part_sent)
    halo_copy(0, NEAR).wait_send()
    await_bytes(outgoing.at[:, NEAR], near_sent)

    @pl.when(has_far)
    def _():
        halo_copy(0, FAR).wait_send()
        await_bytes(outgoing.at[:, FAR], far_sent)

    await_bytes(ghost, ghost_recv)
    grow(0)
    grow(DIRS - 1)
    await_bytes(parts, part_recv)
    whole = (part[...] + parts[0] + parts[1] + parts[2]) * jnp.float32(1.0 / COMPS)
    energy = whole[0:1]
    mean_freq = whole[1:2] / jnp.maximum(energy, 0.05)
    strength = mean_freq * mean_freq * mean_freq * energy * energy
    damping = 0.005 * (sigma * sigma) * strength
    factor = 1.0 / (1.0 + damping)
    for d in range(DIRS):
        span = slice(d * NK, (d + 1) * NK)
        out_ref[span] = gain[span] * factor


def shards(
    row_of_tiles,
    action,
    speed_courant,
    turning,
    freq_shift,
    wind_speed,
    wind_dir,
    sea_mask,
    neighbours,
    halo_rows,
):
    vmem = pltpu.VMEM
    f32 = jnp.float32
    dma = pltpu.SemaphoreType.DMA

    def row(values):
        return values.reshape(1, values.shape[0])

    return pl.pallas_call(
        functools.partial(kernel, row_of_tiles),
        out_shape=pltpu.VMEM((ROWS, PTS), f32),
        in_specs=[pl.BlockSpec(memory_space=pltpu.HBM)] * 9,
        out_specs=pl.BlockSpec(memory_space=pltpu.VMEM),
        scratch_shapes=[
            vmem((ROWS, PTS), f32),
            vmem((1, NK), f32),
            vmem((4, PTS), f32),
            vmem((1, PTS), jnp.int32),
            vmem((4, PTS), jnp.int32),
            vmem((1, 2 * RIM), jnp.int32),
            vmem((EXT, OWN_N), jnp.bfloat16),
            vmem((2, EXT, 2 * RIM), jnp.bfloat16),
            vmem((2, RIM, 2 * RIM), jnp.bfloat16),
            vmem((ROWS, RIM), f32),
            vmem((ROWS, RIM), f32),
            vmem((ROWS, RIM), f32),
            vmem((2, ROWS + SPOT_ROWS, RIM), f32),
            vmem((2, ROWS + SPOT_ROWS, RIM), f32),
            vmem((NSUB - 1, 2, ROWS, RIM), f32),
            vmem((NSUB - 1, 2, ROWS, RIM), f32),
            vmem((ROWS, PTS), f32),
            vmem((2, 2, ROWS, RIM), f32),
            vmem((2, ROWS, RIM), f32),
            vmem((2, ROWS, RIM), f32),
            vmem((ROWS, PTS), f32),
            vmem((2, NK, PTS), f32),
            vmem((2, PTS), f32),
            vmem((3, 2, PTS), f32),
            dma((6,)),
            dma((NSUB, 2)),
            dma,
            dma,
            pltpu.SemaphoreType.REGULAR,
        ],
        compiler_params=pltpu.CompilerParams(
            collective_id=0, has_side_effects=True, vmem_limit_bytes=48 * 1024 * 1024
        ),
        name="wave_step",
    )(
        *(
            pltpu.with_memory_space_constraint(values, pltpu.HBM)
            for values in (
                action,
                row(speed_courant),
                row(turning),
                row(freq_shift),
                row(wind_speed),
                row(wind_dir),
                row(sea_mask),
                neighbours,
                row(halo_rows),
            )
        )
    )


def solution(mesh):
    placed = (
        P("comp", "tiles"),
        P(),
        P("tiles"),
        P("tiles"),
        P("tiles"),
        P("tiles"),
        P("tiles"),
        P(None, "tiles"),
        P("tiles"),
    )
    return jax.shard_map(
        functools.partial(shards, mesh.shape["tiles"] // COMP_AXIS),
        mesh=mesh,
        in_specs=placed,
        out_specs=P("comp", "tiles"),
        check_vma=False,
    )
```

time: 23.8 us -> 23.6 us (level)
  no operation moved by 1% of the time
where the time goes in v4:
time: 23.6 us
  Pallas kernels  22.8 us (97%)
  local copies, waits for them, and re-layouts  0.75 us (3%)
    pallas_call x1, Pallas kernels, shards(): pl.pallas_call(functools.partial(kernel, row_of_tiles), out_shape=pltpu.V...  22.8 us
    unnamed x1, local copies, waits for them, and re-layouts  0.75 us

profile of v4, /device:TPU:6, one launch (start us, length us, event | category | flops | bytes accessed | tf_op | source)
XLA Modules:
  0.0 23.6 jit_solution(8972627501623741547)
XLA Ops:
  0.0 22.8 %wave_step.1 = f32[192,512]{1,0:T(8,128)S(1)} custom-call(f32[192,512]{1,0:T(8,128)} %action_hbm.1, f32[1,32]{1,0:T(1,128)} %bitcast.13, f32[1,512]{1,0:T(1,128)} %bitcast.7, f32[1,512]{1,0:T(1,128)} %bitcast.8, f32[1,512]{1,0:T(1,128)} %bitcast.9, f32[1,512]{1,0:T(1,128)} %bitcast.10, s32[1,512]{1,0:T(1,128)} %bitcast.11, s32[4,512]{1,0:T(4,128)} %links_hbm.1, ...), custom_call_target="tpu_custom_call" | custom-call | tf_op jit(solution)/shard_map/wave_step/pallas_call | solution.py:503
  22.8 0.7 %copy.11 = f32[192,512]{1,0:T(8,128)} copy(f32[192,512]{1,0:T(8,128)S(1)} %wave_step.1) | data formatting | bytes 786432

commit v5 on v4

--- a/solution.py
+++ b/solution.py
@@ -20,8 +20,11 @@
 ROWS = DIRS * NK
 COMPS = NTH * NK
 OWN_N = 2 * PTS
-NEAR, FAR = 0, 1
+NEAR, FAR, LAST_FAR = 0, 1, 2
 SPOT_ROWS = 8
+SUM_ROWS = 16
+ENDS = ((0, NK), (ROWS - NK, ROWS))
+INNER = ((NK, ROWS - NK),)
 MESH = pl.DeviceIdType.MESH
 STEP = np.float32(2.0 * math.pi / NTH)
 LOG_RATIO = np.float32(math.log(1.1))
@@ -44,6 +47,14 @@
     both = jnp.dot(split, table, preferred_element_type=jnp.float32)
     rows = both.shape[0] // 2
     return both[:rows] + both[rows:]
+
+
+def gathered_both(first, second, table):
+    split = jnp.concatenate([halves(first), halves(second)], axis=0)
+    both = jnp.dot(split, table, preferred_element_type=jnp.float32)
+    rows, more = (first.shape[0], second.shape[0])
+    last = both[2 * rows :]
+    return both[:rows] + both[rows : 2 * rows], last[:more] + last[more:]
 
 
 def wide(column, lanes):
@@ -85,16 +96,19 @@
     rim,
     pending,
     pending_send,
-    lists,
     mended,
     gain,
     ghost,
     part,
     parts,
+    sums_out,
+    sums_in,
     local_sem,
     halo_recv,
     ghost_recv,
     part_recv,
+    last_sent,
+    last_recv,
     two_on,
 ):
     tile = lax.axis_index("tiles")
@@ -108,16 +122,17 @@
     comp_at = [lax.rem(comp + step, COMP_AXIS) for step in range(COMP_AXIS)]
 
     barrier = pltpu.get_barrier_semaphore()
+
+    @pl.when(has_far)
+    def _():
+        pl.semaphore_signal(barrier, inc=1, device_id=(far_tile, comp), device_id_type=MESH)
+
     for place in (
         (near_tile, comp),
         (tile, comp_at[1]),
         (tile, comp_at[3]),
     ):
         pl.semaphore_signal(barrier, inc=1, device_id=place, device_id_type=MESH)
-
-    @pl.when(has_far)
-    def _():
-        pl.semaphore_signal(barrier, inc=1, device_id=(far_tile, comp), device_id_type=MESH)
 
     loads = [
         pltpu.make_async_copy(source, target, local_sem.at[number])
@@ -240,6 +255,35 @@
         along[span] = speed_y
         keep[span] = 1.0 - speed_x - speed_y
 
+    number = lax.broadcasted_iota(jnp.int32, (NK, RIM), 0)
+    sigma_rim = jnp.exp((number - NK // 2).astype(jnp.float32) * LOG_RATIO)
+    sigma_up = jnp.exp((number + 1 - NK // 2).astype(jnp.float32) * LOG_RATIO)
+    sigma_down = jnp.exp((number - 1 - NK // 2).astype(jnp.float32) * LOG_RATIO)
+    sigma_up = jnp.where(number == NK - 1, 0.0, sigma_up)
+    sigma_down = jnp.where(number == 0, 0.0, sigma_down)
+    weights = (
+        sigma_rim,
+        sigma_up,
+        sigma_down,
+        sigma_rim * sigma_rim,
+        sigma_up * sigma_up,
+        sigma_down * sigma_down,
+    )
+
+    def sums(values, shares):
+        lanes = values.shape[1]
+        total = wide(shares[0:NK], lanes) * values[0:NK]
+        for d in range(1, DIRS):
+            span = slice(d * NK, (d + 1) * NK)
+            total = total + wide(shares[span], lanes) * values[span]
+        return [
+            jnp.sum(wide(weight, lanes) * total, axis=0, keepdims=True) for weight in weights
+        ]
+
+    def upwind_sums(values):
+        gap = [jnp.zeros((SUM_ROWS // 2 - len(weights), values.shape[1]), jnp.float32)]
+        return jnp.concatenate(sums(values, across) + gap + sums(values, along) + gap, axis=0)
+
     def weighed(picked):
         lanes = picked.shape[1] // 2
         return (
@@ -257,11 +301,10 @@
         pending[...] = wide(keep[...], PTS) * values + from_points(split, OWN)
 
     def own_sends(level, split, side, values):
-        lists[side] = values
         pending_send[level % 2, side] = keep[...] * values + from_sends(split, OWN, side)
 
-    def mend(side):
-        return weighed(gathered(halves(lists[side]), back_table[side]))
+    def mend(side, values):
+        return weighed(gathered(halves(values), back_table[side]))
 
     loads[2].wait()
     spec[...] = spec[...] * wet
@@ -277,6 +320,7 @@
         for level in range(1, NSUB):
             rim[level - 1, FAR] = jnp.zeros((ROWS, RIM), jnp.float32)
         first_rim[FAR, 0:ROWS] = jnp.zeros((ROWS, RIM), jnp.float32)
+        sums_in[...] = jnp.zeros((SUM_ROWS, RIM), jnp.float32)
         first_rim[FAR, ROWS:] = jnp.full((SPOT_ROWS, RIM), float(RIM), jnp.float32)
 
     pl.semaphore_wait(barrier, jnp.where(has_far, 4, 3))
@@ -325,10 +369,7 @@
     send_halo(1, FAR, for_far(0, near_0))
     own_points(split_0, spec[...])
     await_bytes(misc, local_sem.at[5])
-    sigma = jnp.exp(
-        (lax.broadcasted_iota(jnp.int32, (NK, RIM), 0) - NK // 2).astype(jnp.float32) * LOG_RATIO
-    )
-    sigma = wide(sigma, PTS)
+    sigma = wide(sigma_rim, PTS)
     angle = (lax.broadcasted_iota(jnp.int32, (8, PTS), 0) + comp * DIRS).astype(jnp.float32) * STEP
     aligned = jnp.cos(angle - misc[3:4])
     driven = misc[2:3] * sigma
@@ -342,7 +383,7 @@
     points_1 = next_points(both_0)
     send_halo(1, NEAR, near_list_1)
     split_1 = halves(points_1)
-    own_first = lists[FAR]
+    far_list_0 = first_out[FAR, 0:ROWS]
     own_sends(1, split_1, FAR, far_list_1)
     places = lax.broadcasted_iota(jnp.int32, (RIM, RIM), 0).astype(jnp.float32)
     for side in SIDES:
@@ -351,7 +392,7 @@
             back_table[side, :, axis * RIM : (axis + 1) * RIM] = jnp.where(
                 places == spots, 1.0, 0.0
             ).astype(jnp.bfloat16)
-    mended[FAR] = weighed(gathered(halves(own_first), back_table[FAR]))
+    mended[FAR] = mend(FAR, far_list_0)
 
     can_wait = lax.rem(tile, row_of_tiles) == row_of_tiles - 1
 
@@ -384,51 +425,104 @@
     points_2 = wide(keep[...], PTS) * points_1 + from_points(joined(split_1, both_1), slice(0, EXT))
     far_list_2 = whole_list(1, FAR, both_1)
     split_2 = halves(points_2)
-    far_share = mend(FAR)
-    mended[FAR] = far_share
     own_sends(2, split_2, FAR, far_list_2)
-    lists[NEAR] = near_list_1
-    mended[NEAR] = mend(NEAR)
-
+    mended[NEAR] = mend(NEAR, near_list_1)
+
+    def last_copy(first, past):
+        inner = first > 0 and past < ROWS
+        span = pl.ds(first, past - first)
+        return pltpu.make_async_remote_copy(
+            src_ref=outgoing.at[2, FAR, span],
+            dst_ref=rim.at[2, FAR, span],
+            send_sem=far_sent,
+            recv_sem=last_recv.at[0] if inner else halo_recv.at[3, FAR],
+            device_id=(far_tile, comp),
+            device_id_type=MESH,
+        )
+
+    sums_copy = pltpu.make_async_remote_copy(
+        src_ref=sums_out,
+        dst_ref=sums_in,
+        send_sem=last_sent,
+        recv_sem=last_recv.at[1],
+        device_id=(far_tile, comp),
+        device_id_type=MESH,
+    )
     near_2 = arrived(2, NEAR)
-    send_halo(3, FAR, for_far(2, near_2))
+    far_sends = for_far(2, near_2)
+    outgoing[2, FAR] = far_sends
+    for first, past in ENDS:
+        only_if_far(FAR, lambda: last_copy(first, past).start())
+    sums_out[...] = upwind_sums(far_sends)
+    only_if_far(FAR, lambda: sums_copy.start())
+    for first, past in INNER:
+        only_if_far(FAR, lambda: last_copy(first, past).start())
 
     @pl.when(can_wait)
     def _():
         near_list_work()
         send_halo(2, NEAR, pending_send[1, NEAR] + from_sends(far_1, FAR_ROWS, NEAR))
 
+    mended[FAR] = mend(FAR, far_list_1)
     own_sends(2, split_2, NEAR, whole_list(1, NEAR, both_1))
     own_points(split_2, points_2)
+    mended[LAST_FAR] = mend(FAR, far_list_2)
+    mended_sums = upwind_sums(mended[LAST_FAR])
     both_2 = joined(near_2, arrived(2, FAR))
-    near_list_3 = whole_list(2, NEAR, both_2)
+    send_halo(3, NEAR, whole_list(2, NEAR, both_2))
     points_3 = next_points(both_2)
-    send_halo(3, NEAR, near_list_3)
-    own_points(halves(points_3), points_3)
-    mended[FAR] = mend(FAR)
-
-    near_3 = arrived(3, NEAR)
-    spec[...] = next_points(joined(near_3, arrived(3, FAR)))
-    for copy in ghost_copies:
-        copy.start()
+
+    def chosen(values, spans):
+        return jnp.concatenate([values[first:past] for first, past in spans], axis=0)
+
+    def weighed_at(spans, picked):
+        return (
+            wide(chosen(across[...], spans), PTS) * picked[:, :PTS]
+            + wide(chosen(along[...], spans), PTS) * picked[:, PTS:]
+        )
+
+    ends_picked, own_sums = gathered_both(
+        chosen(points_3, ENDS), upwind_sums(points_3), table[OWN, :]
+    )
+    ends_own = wide(chosen(keep[...], ENDS), PTS) * chosen(points_3, ENDS) + weighed_at(
+        ENDS, ends_picked
+    )
+    kept_sums = sums(points_3, keep)
+
+    def rims_of(spans):
+        near = [rim[2, NEAR, first:past] for first, past in spans]
+        far = [
+            rim[2, FAR, first:past] + mended[LAST_FAR, first:past] for first, past in spans
+        ]
+        return joined(jnp.concatenate(near, axis=0), jnp.concatenate(far, axis=0))
+
+    await_halo(3, NEAR)
+
+    @pl.when(has_far)
+    def _():
+        sums_copy.wait_recv()
+        await_bytes(rim.at[2, FAR, pl.ds(0, 2 * NK)], halo_recv.at[3, FAR])
 
     turn = misc[0:1]
     moved = misc[1:2]
-    freq = lax.broadcasted_iota(jnp.int32, (NK, PTS), 0)
-
-    def shifted(values):
-        lower = jnp.where(freq == 0, 0.0, pltpu.roll(values, 1, 0))
-        upper = jnp.where(freq == NK - 1, 0.0, pltpu.roll(values, NK - 1, 0))
-        return values - jnp.abs(moved) * (values - jnp.where(moved > 0, lower, upper))
-
-    total = spec[0:NK]
-    for d in range(1, DIRS):
-        total = total + spec[d * NK : (d + 1) * NK]
-    total = shifted(total) * sigma
-    energy = jnp.sum(total, axis=0, keepdims=True)
-    moment = jnp.sum(total * sigma, axis=0, keepdims=True)
-    part[0:1] = energy
-    part[1:2] = moment
+    rim_sums = jnp.concatenate([upwind_sums(rim[2, NEAR]), sums_in[...] + mended_sums], axis=1)
+    ends_picked, rim_sums = gathered_both(rims_of(ENDS), rim_sums, table[RIMS, :])
+    ends = ends_own + weighed_at(ENDS, ends_picked)
+    upwind = own_sums + rim_sums
+    across_sums = upwind[0 : SUM_ROWS // 2, :PTS]
+    along_sums = upwind[SUM_ROWS // 2 :, PTS:]
+    point_sums = [
+        kept + across_sums[at : at + 1] + along_sums[at : at + 1]
+        for at, kept in enumerate(kept_sums)
+    ]
+
+    def after_shift(still, up, down):
+        return still - jnp.abs(moved) * (still - jnp.where(moved > 0, up, down))
+
+    part[0:1] = after_shift(*point_sums[0:3])
+    part[1:2] = after_shift(*point_sums[3:6])
+    spec[0:NK] = ends[:NK]
+    spec[ROWS - NK :] = ends[NK:]
     part_copies = [
         pltpu.make_async_remote_copy(
             src_ref=part,
@@ -441,8 +535,21 @@
         for hop in (2, 1, 3)
     ]
     pl.semaphore_wait(two_on, 1)
-    for copy in part_copies:
+    for copy in part_copies + ghost_copies:
         copy.start()
+    only_if_far(FAR, lambda: last_copy(*INNER[0]).wait_recv())
+    inner = chosen(points_3, INNER)
+    inner_picked = gathered(halves(joined(inner, rims_of(INNER))), table[...])
+    spec[NK : ROWS - NK] = wide(chosen(keep[...], INNER), PTS) * inner + weighed_at(
+        INNER, inner_picked
+    )
+
+    freq = lax.broadcasted_iota(jnp.int32, (NK, PTS), 0)
+
+    def shifted(values):
+        lower = jnp.where(freq == 0, 0.0, pltpu.roll(values, 1, 0))
+        upper = jnp.where(freq == NK - 1, 0.0, pltpu.roll(values, NK - 1, 0))
+        return values - jnp.abs(moved) * (values - jnp.where(moved > 0, lower, upper))
 
     def refracted(d):
         values = spec[d * NK : (d + 1) * NK]
@@ -450,12 +557,11 @@
         beyond = ghost[1] if d == DIRS - 1 else spec[(d + 1) * NK : (d + 2) * NK]
         return values - jnp.abs(turn) * (values - jnp.where(turn > 0, before, beyond))
 
-    def grow(d):
-        span = slice(d * NK, (d + 1) * NK)
-        gain[span] = gain[span] * shifted(refracted(d))
+    def grown(d):
+        return gain[d * NK : (d + 1) * NK] * shifted(refracted(d))
 
     for d in range(1, DIRS - 1):
-        grow(d)
+        gain[d * NK : (d + 1) * NK] = grown(d)
     await_bytes(ghost, ghost_sent)
     await_bytes(parts, part_sent)
     halo_copy(0, NEAR).wait_send()
@@ -465,10 +571,8 @@
     def _():
         halo_copy(0, FAR).wait_send()
         await_bytes(outgoing.at[:, FAR], far_sent)
-
-    await_bytes(ghost, ghost_recv)
-    grow(0)
-    grow(DIRS - 1)
+        sums_copy.wait_send()
+
     await_bytes(parts, part_recv)
     whole = (part[...] + parts[0] + parts[1] + parts[2]) * jnp.float32(1.0 / COMPS)
     energy = whole[0:1]
@@ -476,9 +580,14 @@
     strength = mean_freq * mean_freq * mean_freq * energy * energy
     damping = 0.005 * (sigma * sigma) * strength
     factor = 1.0 / (1.0 + damping)
-    for d in range(DIRS):
+    for d in range(1, DIRS - 1):
         span = slice(d * NK, (d + 1) * NK)
         out_ref[span] = gain[span] * factor
+    for first, past in ENDS:
+        gain[first:past] = gain[first:past] * factor
+    await_bytes(ghost, ghost_recv)
+    for d in (0, DIRS - 1):
+        out_ref[d * NK : (d + 1) * NK] = grown(d)
 
 
 def shards(
@@ -524,16 +633,19 @@
             vmem((NSUB - 1, 2, ROWS, RIM), f32),
             vmem((ROWS, PTS), f32),
             vmem((2, 2, ROWS, RIM), f32),
-            vmem((2, ROWS, RIM), f32),
-            vmem((2, ROWS, RIM), f32),
+            vmem((3, ROWS, RIM), f32),
             vmem((ROWS, PTS), f32),
             vmem((2, NK, PTS), f32),
             vmem((2, PTS), f32),
             vmem((3, 2, PTS), f32),
+            vmem((SUM_ROWS, RIM), f32),
+            vmem((SUM_ROWS, RIM), f32),
             dma((6,)),
             dma((NSUB, 2)),
             dma,
             dma,
+            dma,
+            dma((2,)),
             pltpu.SemaphoreType.REGULAR,
         ],
         compiler_params=pltpu.CompilerParams(

time: 23.6 us -> 23.5 us (level)
    pallas_call x1, Pallas kernels: 22.8 us -> 22.6 us  [shards(): pl.pallas_call(functools.partial(kernel, row_of_tiles), out_shape=pltpu.V...]
where the time goes in v5:
time: 23.5 us; the launch traced here: 23.3 us
  Pallas kernels  22.6 us (96%)
  local copies, waits for them, and re-layouts  0.75 us (3%)
    pallas_call x1, Pallas kernels, shards(): pl.pallas_call(functools.partial(kernel, row_of_tiles), out_shape=pltpu.V...  22.6 us
    unnamed x1, local copies, waits for them, and re-layouts  0.75 us

profile of v5, /device:TPU:6, one launch (start us, length us, event | category | flops | bytes accessed | tf_op | source)
XLA Modules:
  0.0 23.3 jit_solution(8120241055847171079)
XLA Ops:
  0.0 22.6 %wave_step.1 = f32[192,512]{1,0:T(8,128)S(1)} custom-call(f32[192,512]{1,0:T(8,128)} %action_hbm.1, f32[1,32]{1,0:T(1,128)} %bitcast.13, f32[1,512]{1,0:T(1,128)} %bitcast.7, f32[1,512]{1,0:T(1,128)} %bitcast.8, f32[1,512]{1,0:T(1,128)} %bitcast.9, f32[1,512]{1,0:T(1,128)} %bitcast.10, s32[1,512]{1,0:T(1,128)} %bitcast.11, s32[4,512]{1,0:T(4,128)} %links_hbm.1, ...), custom_call_target="tpu_custom_call" | custom-call | tf_op jit(solution)/shard_map/wave_step/pallas_call | solution.py:612
  22.6 0.7 %copy.11 = f32[192,512]{1,0:T(8,128)} copy(f32[192,512]{1,0:T(8,128)S(1)} %wave_step.1) | data formatting | bytes 786432

commit v6 on v5

--- a/solution.py
+++ b/solution.py
@@ -323,6 +323,7 @@
         sums_in[...] = jnp.zeros((SUM_ROWS, RIM), jnp.float32)
         first_rim[FAR, ROWS:] = jnp.full((SPOT_ROWS, RIM), float(RIM), jnp.float32)
 
+    mended[FAR] = jnp.zeros((ROWS, RIM), jnp.float32)
     pl.semaphore_wait(barrier, jnp.where(has_far, 4, 3))
     for side in SIDES:
         only_if_far(side, lambda: halo_copy(0, side).start())
@@ -383,16 +384,19 @@
     points_1 = next_points(both_0)
     send_halo(1, NEAR, near_list_1)
     split_1 = halves(points_1)
-    far_list_0 = first_out[FAR, 0:ROWS]
     own_sends(1, split_1, FAR, far_list_1)
-    places = lax.broadcasted_iota(jnp.int32, (RIM, RIM), 0).astype(jnp.float32)
-    for side in SIDES:
-        for axis in range(2):
-            spots = first_rim[side, ROWS + axis : ROWS + axis + 1]
-            back_table[side, :, axis * RIM : (axis + 1) * RIM] = jnp.where(
-                places == spots, 1.0, 0.0
-            ).astype(jnp.bfloat16)
-    mended[FAR] = mend(FAR, far_list_0)
+
+    def far_share():
+        places = lax.broadcasted_iota(jnp.int32, (RIM, RIM), 0).astype(jnp.float32)
+        for side in SIDES:
+            for axis in range(2):
+                spots = first_rim[side, ROWS + axis : ROWS + axis + 1]
+                back_table[side, :, axis * RIM : (axis + 1) * RIM] = jnp.where(
+                    places == spots, 1.0, 0.0
+                ).astype(jnp.bfloat16)
+        mended[FAR] = mend(FAR, first_out[FAR, 0:ROWS])
+
+    pl.when(first_core)(far_share)
 
     can_wait = lax.rem(tile, row_of_tiles) == row_of_tiles - 1
 
@@ -417,6 +421,7 @@
 
     await_side(first_side)
     send_past(first_side)
+    pl.when(jnp.logical_not(first_core))(far_share)
     await_side(1 - first_side)
     pl.when(jnp.logical_not(can_wait))(lambda: send_past(1 - first_side))
     near_1 = halves(whole_rim(1, NEAR))

time: 23.5 us -> 23.5 us (level)
  no operation moved by 1% of the time
where the time goes in v6:
time: 23.5 us; the launch traced here: 23.3 us
  Pallas kernels  22.6 us (96%)
  local copies, waits for them, and re-layouts  0.75 us (3%)
    pallas_call x1, Pallas kernels, shards(): pl.pallas_call(functools.partial(kernel, row_of_tiles), out_shape=pltpu.V...  22.6 us
    unnamed x1, local copies, waits for them, and re-layouts  0.75 us

profile of v6, /device:TPU:6, one launch (start us, length us, event | category | flops | bytes accessed | tf_op | source)
XLA Modules:
  0.0 23.3 jit_solution(9234409331185845182)
XLA Ops:
  0.0 22.6 %wave_step.1 = f32[192,512]{1,0:T(8,128)S(1)} custom-call(f32[192,512]{1,0:T(8,128)} %action_hbm.1, f32[1,32]{1,0:T(1,128)} %bitcast.13, f32[1,512]{1,0:T(1,128)} %bitcast.7, f32[1,512]{1,0:T(1,128)} %bitcast.8, f32[1,512]{1,0:T(1,128)} %bitcast.9, f32[1,512]{1,0:T(1,128)} %bitcast.10, s32[1,512]{1,0:T(1,128)} %bitcast.11, s32[4,512]{1,0:T(4,128)} %links_hbm.1, ...), custom_call_target="tpu_custom_call" | custom-call | tf_op jit(solution)/shard_map/wave_step/pallas_call | solution.py:617
  22.6 0.7 %copy.11 = f32[192,512]{1,0:T(8,128)} copy(f32[192,512]{1,0:T(8,128)S(1)} %wave_step.1) | data formatting | bytes 786432

commit v7 on v5

--- a/solution.py
+++ b/solution.py
@@ -107,7 +107,6 @@
     halo_recv,
     ghost_recv,
     part_recv,
-    last_sent,
     last_recv,
     two_on,
 ):
@@ -443,7 +442,7 @@
     sums_copy = pltpu.make_async_remote_copy(
         src_ref=sums_out,
         dst_ref=sums_in,
-        send_sem=last_sent,
+        send_sem=first_near_sent,
         recv_sem=last_recv.at[1],
         device_id=(far_tile, comp),
         device_id_type=MESH,
@@ -453,6 +452,7 @@
     outgoing[2, FAR] = far_sends
     for first, past in ENDS:
         only_if_far(FAR, lambda: last_copy(first, past).start())
+    halo_copy(0, NEAR).wait_send()
     sums_out[...] = upwind_sums(far_sends)
     only_if_far(FAR, lambda: sums_copy.start())
     for first, past in INNER:
@@ -564,7 +564,6 @@
         gain[d * NK : (d + 1) * NK] = grown(d)
     await_bytes(ghost, ghost_sent)
     await_bytes(parts, part_sent)
-    halo_copy(0, NEAR).wait_send()
     await_bytes(outgoing.at[:, NEAR], near_sent)
 
     @pl.when(has_far)
@@ -644,7 +643,6 @@
             dma((NSUB, 2)),
             dma,
             dma,
-            dma,
             dma((2,)),
             pltpu.SemaphoreType.REGULAR,
         ],

time: 23.5 us -> 23.5 us (level)
  no operation moved by 1% of the time
where the time goes in v7:
time: 23.5 us; the launch traced here: 23.3 us
  Pallas kernels  22.5 us (96%)
  local copies, waits for them, and re-layouts  0.75 us (3%)
    pallas_call x1, Pallas kernels, shards(): pl.pallas_call(functools.partial(kernel, row_of_tiles), out_shape=pltpu.V...  22.5 us
    unnamed x1, local copies, waits for them, and re-layouts  0.75 us

profile of v7, /device:TPU:6, one launch (start us, length us, event | category | flops | bytes accessed | tf_op | source)
XLA Modules:
  0.0 23.3 jit_solution(10251766407551197588)
XLA Ops:
  0.0 22.5 %wave_step.1 = f32[192,512]{1,0:T(8,128)S(1)} custom-call(f32[192,512]{1,0:T(8,128)} %action_hbm.1, f32[1,32]{1,0:T(1,128)} %bitcast.13, f32[1,512]{1,0:T(1,128)} %bitcast.7, f32[1,512]{1,0:T(1,128)} %bitcast.8, f32[1,512]{1,0:T(1,128)} %bitcast.9, f32[1,512]{1,0:T(1,128)} %bitcast.10, s32[1,512]{1,0:T(1,128)} %bitcast.11, s32[4,512]{1,0:T(4,128)} %links_hbm.1, ...), custom_call_target="tpu_custom_call" | custom-call | tf_op jit(solution)/shard_map/wave_step/pallas_call | solution.py:611
  22.6 0.7 %copy.11 = f32[192,512]{1,0:T(8,128)} copy(f32[192,512]{1,0:T(8,128)S(1)} %wave_step.1) | data formatting | bytes 786432
